TPU v7x, 128 devices: a whole 4x4x4 slice. The times are simulated.
128 devices in a mesh: fsdp: 16 (over x_lo, y, core), dp: 8 (over x_hi, z).
Axes of the slice: x: 4 (x_hi: 2, x_lo: 2; x = x_hi * 2 + x_lo), y: 4, z: 4, core: 2. Of those that a mesh axis runs over, the one named last changes fastest.
Arguments:
- tokens: bfloat16 [16, 1024, 2048], P('fsdp', 'dp'), may hold values from -6 to 6
- segment_ids: int32 [16, 1024], P('fsdp'), may hold values from -1 to 2, as said below
- out_cotangent: bfloat16 [16, 1024, 2048], P('fsdp', 'dp'), may hold values from -6 to 6
- ln1_gain: bfloat16 [2048], P('fsdp'), may hold values from 0.5 to 1.5
- ln1_bias: bfloat16 [2048], P('fsdp'), may hold values from -1.1953125 to 1.1953125
- qkv_weight: bfloat16 [2048, 6144], P('fsdp'), may hold values from -0.125 to 0.125
- qkv_bias: bfloat16 [6144], P('fsdp'), may hold values from -0.59765625 to 0.59765625
- out_weight: bfloat16 [2048, 2048], P('fsdp'), may hold values from -1 to 1
- out_bias: bfloat16 [2048], P('fsdp'), may hold values from -1.1953125 to 1.1953125
- ln2_gain: bfloat16 [2048], P('fsdp'), may hold values from 0.5 to 1.5
- ln2_bias: bfloat16 [2048], P('fsdp'), may hold values from -1.1953125 to 1.1953125
- up_weight: bfloat16 [2048, 8192], P('fsdp'), may hold values from -0.125 to 0.125
- up_bias: bfloat16 [8192], P('fsdp'), may hold values from -1.1953125 to 1.1953125
- down_weight: bfloat16 [8192, 2048], P('fsdp'), may hold values from -0.0625 to 0.0625
- down_bias: bfloat16 [2048], P('fsdp'), may hold values from -1.1953125 to 1.1953125
Outputs:
- layer_output: bfloat16 [16, 1024, 2048], P('fsdp', 'dp')
- input_grad: bfloat16 [16, 1024, 2048], P('fsdp', 'dp')
- grad_ln1_gain: float32 [2048], P('fsdp')
- grad_ln1_bias: float32 [2048], P('fsdp')
- grad_qkv_weight: float32 [2048, 6144], P('fsdp')
- grad_qkv_bias: float32 [6144], P('fsdp')
- grad_out_weight: float32 [2048, 2048], P('fsdp')
- grad_out_bias: float32 [2048], P('fsdp')
- grad_ln2_gain: float32 [2048], P('fsdp')
- grad_ln2_bias: float32 [2048], P('fsdp')
- grad_up_weight: float32 [2048, 8192], P('fsdp')
- grad_up_bias: float32 [8192], P('fsdp')
- grad_down_weight: float32 [8192, 2048], P('fsdp')
- grad_down_bias: float32 [2048], P('fsdp')
Inputs may be any that keep to these rules, and one draw needn't show every extreme that they name: `segment_ids`: each packed sequence holds, in order, document 0 of fewer than 128 positions, document 1, document 2 of fewer than 64 positions, and fewer than 64 padding positions marked -1; each of the four runs is nonempty.
All inputs are finite; a program needn't handle non-finite values.
Results may differ from a plain program's by a relative error of at most 0.02.
Values may be sent and summed in bfloat16 or wider, within the bound.
No kernel may reach another device: no remote copies, remote signals or barrier semaphores. Data moves between devices by JAX's collectives and lax.ppermute only.
A program may use at most 448 MiB of HBM per device.

v0:
```python
import math

import jax
import jax.numpy as jnp
from jax import lax
from jax.sharding import PartitionSpec as P

HEADS = 8
ROTARY = 64


norm_eps = 1e-05
masked_score = -1e30


def layer_norm(values, gain_vec, shift_vec):
    center = values - jnp.mean(values, axis=-1, keepdims=True)
    spread = jnp.mean(center * center, axis=-1, keepdims=True)
    return center * lax.rsqrt(spread + norm_eps) * gain_vec + shift_vec


def rotary_tables(places, rotary):
    half_dims = rotary // 2
    freqs = jnp.exp(jnp.arange(half_dims, dtype=jnp.float32) * (-2.0 * math.log(10000.0) / rotary))
    angles = places.astype(jnp.float32)[:, None] * freqs[None, :]
    return (jnp.cos(angles), jnp.sin(angles))


def rotate(head_vals, rot_cos, rot_sin, rotary):
    half_dims = rotary // 2
    front_half = head_vals[..., :half_dims]
    back_half = head_vals[..., half_dims:rotary]
    return jnp.concatenate(
        [
            front_half * rot_cos - back_half * rot_sin,
            back_half * rot_cos + front_half * rot_sin,
            head_vals[..., rotary:],
        ],
        axis=-1,
    )


def gelu_exact(values):
    return jax.nn.gelu(values, approximate=False)


def owner_sums(terms):
    owned = (
        lax.psum_scatter(
            terms[0].astype(jnp.bfloat16), "fsdp", scatter_dimension=0, tiled=True
        ).astype(jnp.float32),
        lax.psum_scatter(
            terms[1].astype(jnp.bfloat16), "fsdp", scatter_dimension=0, tiled=True
        ).astype(jnp.float32),
        lax.psum_scatter(
            terms[2].astype(jnp.bfloat16), "fsdp", scatter_dimension=0, tiled=True
        ).astype(jnp.float32),
        lax.psum_scatter(
            terms[3].astype(jnp.bfloat16), "fsdp", scatter_dimension=0, tiled=True
        ).astype(jnp.float32),
        lax.psum_scatter(
            terms[4].astype(jnp.bfloat16), "fsdp", scatter_dimension=0, tiled=True
        ).astype(jnp.float32),
        lax.psum_scatter(
            terms[5].astype(jnp.bfloat16), "fsdp", scatter_dimension=0, tiled=True
        ).astype(jnp.float32),
    )
    return (
        lax.psum(owned[0].astype(jnp.bfloat16), "dp").astype(jnp.float32),
        lax.psum(owned[1].astype(jnp.bfloat16), "dp").astype(jnp.float32),
        lax.psum(owned[2].astype(jnp.bfloat16), "dp").astype(jnp.float32),
        lax.psum(owned[3].astype(jnp.bfloat16), "dp").astype(jnp.float32),
        lax.psum(owned[4].astype(jnp.bfloat16), "dp").astype(jnp.float32),
        lax.psum(owned[5].astype(jnp.bfloat16), "dp").astype(jnp.float32),
    )


def body(
    tokens,
    segment_ids,
    out_cotangent,
    ln1_gain,
    ln1_bias,
    qkv_weight,
    qkv_bias,
    out_weight,
    out_bias,
    ln2_gain,
    ln2_bias,
    up_weight,
    up_bias,
    down_weight,
    down_bias,
):
    pack_count, shard_len, model_width = tokens.shape
    seq_len = segment_ids.shape[1]
    head_count = HEADS
    head_dim = model_width // head_count
    row_count = pack_count * shard_len
    score_scale = head_dim ** (-0.5)
    gathered = (
        lax.all_gather(ln1_gain, "fsdp", axis=0, tiled=True),
        lax.all_gather(ln1_bias, "fsdp", axis=0, tiled=True),
        lax.all_gather(qkv_weight, "fsdp", axis=0, tiled=True),
        lax.all_gather(qkv_bias, "fsdp", axis=0, tiled=True),
        lax.all_gather(out_weight, "fsdp", axis=0, tiled=True),
        lax.all_gather(out_bias, "fsdp", axis=0, tiled=True),
        lax.all_gather(ln2_gain, "fsdp", axis=0, tiled=True),
        lax.all_gather(ln2_bias, "fsdp", axis=0, tiled=True),
        lax.all_gather(up_weight, "fsdp", axis=0, tiled=True),
        lax.all_gather(up_bias, "fsdp", axis=0, tiled=True),
        lax.all_gather(down_weight, "fsdp", axis=0, tiled=True),
        lax.all_gather(down_bias, "fsdp", axis=0, tiled=True),
    )
    (
        gain_one,
        bias_one,
        w_qkv,
        b_qkv,
        w_out,
        b_out,
        gain_two,
        bias_two,
        w_up,
        b_up,
        w_down,
        b_down,
    ) = gathered
    inputs = tokens.reshape(row_count, model_width).astype(jnp.float32)
    normed_one = layer_norm(
        inputs, gain_one.astype(jnp.float32), bias_one.astype(jnp.float32)
    ).astype(jnp.bfloat16)
    mixed = jnp.dot(normed_one, w_qkv, preferred_element_type=jnp.float32) + b_qkv.astype(
        jnp.float32
    )
    start_place = lax.axis_index("dp") * shard_len
    places = start_place + jnp.arange(shard_len, dtype=jnp.int32)
    rot_cos, rot_sin = rotary_tables(places, ROTARY)
    rot_cos = rot_cos[None, :, None, :]
    rot_sin = rot_sin[None, :, None, :]
    head_shape = (pack_count, shard_len, head_count, head_dim)
    query = rotate(mixed[:, :model_width].reshape(head_shape), rot_cos, rot_sin, ROTARY).astype(
        jnp.bfloat16
    )
    key_vals = rotate(
        mixed[:, model_width : 2 * model_width].reshape(head_shape), rot_cos, rot_sin, ROTARY
    ).astype(jnp.bfloat16)
    value_vals = mixed[:, 2 * model_width :].astype(jnp.bfloat16)
    keys_all, values_all = (
        lax.all_gather(
            key_vals.reshape(pack_count, shard_len, model_width), "dp", axis=1, tiled=True
        ),
        lax.all_gather(
            value_vals.reshape(pack_count, shard_len, model_width), "dp", axis=1, tiled=True
        ),
    )
    full_shape = (pack_count, seq_len, head_count, head_dim)
    keys_all = keys_all.reshape(full_shape)
    values_all = values_all.reshape(full_shape)
    own_ids = lax.dynamic_slice_in_dim(segment_ids, start_place, shard_len, 1)
    key_places = jnp.arange(seq_len, dtype=jnp.int32)
    allowed = (own_ids[:, :, None] == segment_ids[:, None, :]) & (segment_ids[:, None, :] >= 0) & (
        key_places[None, None, :] <= places[None, :, None]
    ) | (key_places[None, None, :] == places[None, :, None])
    allowed = allowed[:, None]

    def attention_scores():
        raw_scores = (
            jnp.einsum("pqhd,pkhd->phqk", query, keys_all, preferred_element_type=jnp.float32)
            * score_scale
        )
        return jnp.where(allowed, raw_scores, masked_score)

    scores = attention_scores()
    top_score = jnp.max(scores, axis=-1, keepdims=True)
    expo = jnp.exp(scores - top_score)
    total = jnp.sum(expo, axis=-1, keepdims=True)
    log_total = top_score + jnp.log(total)
    prob_low = (expo / total).astype(jnp.bfloat16)
    attended = (
        jnp.einsum("phqk,pkhd->pqhd", prob_low, values_all, preferred_element_type=jnp.float32)
        .reshape(row_count, model_width)
        .astype(jnp.bfloat16)
    )
    branch_attn = jnp.dot(attended, w_out, preferred_element_type=jnp.float32) + b_out.astype(
        jnp.float32
    )
    normed_two = layer_norm(
        inputs, gain_two.astype(jnp.float32), bias_two.astype(jnp.float32)
    ).astype(jnp.bfloat16)
    pre_act = jnp.dot(normed_two, w_up, preferred_element_type=jnp.float32) + b_up.astype(
        jnp.float32
    )
    activ = gelu_exact(pre_act).astype(jnp.bfloat16)
    branch_ffn = jnp.dot(activ, w_down, preferred_element_type=jnp.float32) + b_down.astype(
        jnp.float32
    )
    layer_output = (
        (inputs + branch_attn + branch_ffn)
        .astype(jnp.bfloat16)
        .reshape(pack_count, shard_len, model_width)
    )
    grad_out = out_cotangent.reshape(row_count, model_width)
    grad_out_wide = grad_out.astype(jnp.float32)
    zero_shift = jnp.zeros((model_width,), jnp.float32)
    gain_two_again, w_up_again, w_down_again = (
        lax.all_gather(ln2_gain, "fsdp", axis=0, tiled=True),
        lax.all_gather(up_weight, "fsdp", axis=0, tiled=True),
        lax.all_gather(down_weight, "fsdp", axis=0, tiled=True),
    )
    grad_activ = jnp.dot(grad_out, w_down_again.T, preferred_element_type=jnp.float32)
    _, gelu_back = jax.vjp(gelu_exact, pre_act)
    grad_pre = gelu_back(grad_activ)[0].astype(jnp.bfloat16)
    grad_down = jnp.dot(activ.T, grad_out, preferred_element_type=jnp.float32)
    grad_down_bias = jnp.sum(grad_out_wide, axis=0)
    grad_up = jnp.dot(normed_two.T, grad_pre, preferred_element_type=jnp.float32)
    grad_up_bias = jnp.sum(grad_pre.astype(jnp.float32), axis=0)
    grad_normed_two = jnp.dot(grad_pre, w_up_again.T, preferred_element_type=jnp.float32)
    _, norm_two_back = jax.vjp(layer_norm, inputs, gain_two_again.astype(jnp.float32), zero_shift)
    grad_in_two, grad_gain_two, grad_bias_two = norm_two_back(grad_normed_two)
    ffn_grads = owner_sums(
        (grad_gain_two, grad_bias_two, grad_up, grad_up_bias, grad_down, grad_down_bias)
    )
    gain_one_again, w_qkv_again, w_out_again = (
        lax.all_gather(ln1_gain, "fsdp", axis=0, tiled=True),
        lax.all_gather(qkv_weight, "fsdp", axis=0, tiled=True),
        lax.all_gather(out_weight, "fsdp", axis=0, tiled=True),
    )
    grad_attended = jnp.dot(grad_out, w_out_again.T, preferred_element_type=jnp.float32).astype(
        jnp.bfloat16
    )
    grad_out_proj = jnp.dot(attended.T, grad_out, preferred_element_type=jnp.float32)
    grad_attended_heads = grad_attended.reshape(head_shape)
    prob_again = jnp.exp(attention_scores() - log_total)
    grad_values = jnp.einsum(
        "phqk,pqhd->pkhd",
        prob_again.astype(jnp.bfloat16),
        grad_attended_heads,
        preferred_element_type=jnp.float32,
    )
    grad_prob = jnp.einsum(
        "pqhd,pkhd->phqk", grad_attended_heads, values_all, preferred_element_type=jnp.float32
    )
    inner = jnp.sum(prob_again * grad_prob, axis=-1, keepdims=True)
    grad_scores = (prob_again * (grad_prob - inner)).astype(jnp.bfloat16)
    grad_query = (
        jnp.einsum("phqk,pkhd->pqhd", grad_scores, keys_all, preferred_element_type=jnp.float32)
        * score_scale
    )
    grad_keys = (
        jnp.einsum("phqk,pqhd->pkhd", grad_scores, query, preferred_element_type=jnp.float32)
        * score_scale
    )
    key_sum, value_sum = (
        lax.psum_scatter(
            grad_keys.reshape(pack_count, seq_len, model_width).astype(jnp.bfloat16),
            "dp",
            scatter_dimension=1,
            tiled=True,
        ).astype(jnp.float32),
        lax.psum_scatter(
            grad_values.reshape(pack_count, seq_len, model_width).astype(jnp.bfloat16),
            "dp",
            scatter_dimension=1,
            tiled=True,
        ).astype(jnp.float32),
    )
    grad_query_raw = rotate(grad_query, rot_cos, -rot_sin, ROTARY).reshape(row_count, model_width)
    grad_key_raw = rotate(key_sum.reshape(head_shape), rot_cos, -rot_sin, ROTARY).reshape(
        row_count, model_width
    )
    grad_mixed = jnp.concatenate(
        [grad_query_raw, grad_key_raw, value_sum.reshape(row_count, model_width)], axis=1
    ).astype(jnp.bfloat16)
    grad_qkv = jnp.dot(normed_one.T, grad_mixed, preferred_element_type=jnp.float32)
    grad_qkv_bias = jnp.sum(grad_mixed.astype(jnp.float32), axis=0)
    grad_normed_one = jnp.dot(grad_mixed, w_qkv_again.T, preferred_element_type=jnp.float32)
    _, norm_one_back = jax.vjp(layer_norm, inputs, gain_one_again.astype(jnp.float32), zero_shift)
    grad_in_one, grad_gain_one, grad_bias_one = norm_one_back(grad_normed_one)
    attn_grads = owner_sums(
        (grad_gain_one, grad_bias_one, grad_qkv, grad_qkv_bias, grad_out_proj, grad_down_bias)
    )
    input_grad = (
        (grad_out_wide + grad_in_one + grad_in_two)
        .astype(jnp.bfloat16)
        .reshape(pack_count, shard_len, model_width)
    )
    return (
        layer_output,
        input_grad,
        attn_grads[0],
        attn_grads[1],
        attn_grads[2],
        attn_grads[3],
        attn_grads[4],
        attn_grads[5],
        ffn_grads[0],
        ffn_grads[1],
        ffn_grads[2],
        ffn_grads[3],
        ffn_grads[4],
        ffn_grads[5],
    )


def solution(mesh):
    return jax.shard_map(
        body,
        mesh=mesh,
        in_specs=(
            P("fsdp", "dp", None),
            P("fsdp", None),
            P("fsdp", "dp", None),
            P("fsdp"),
            P("fsdp"),
            P("fsdp", None),
            P("fsdp"),
            P("fsdp", None),
            P("fsdp"),
            P("fsdp"),
            P("fsdp"),
            P("fsdp", None),
            P("fsdp"),
            P("fsdp", None),
            P("fsdp"),
        ),
        out_specs=(
            P("fsdp", "dp", None),
            P("fsdp", "dp", None),
            P("fsdp"),
            P("fsdp"),
            P("fsdp", None),
            P("fsdp"),
            P("fsdp", None),
            P("fsdp"),
            P("fsdp"),
            P("fsdp"),
            P("fsdp", None),
            P("fsdp"),
            P("fsdp", None),
            P("fsdp"),
        ),
        check_vma=False,
    )
```

profile of v0, /device:TPU:8, one launch (start us, length us, event | category | flops | bytes accessed | tf_op | source)
XLA Modules:
  0.0 1656.9 jit_solution(11715501649145102499)
XLA Ops:
  26.3 19.4 %all-gather.2 = bf16[16,1,128]{2,1,0:T(2,128)(2,1)S(1)} all-gather(bf16[1,1,128]{2,1,0:T(2,128)(2,1)} %bitcast.232), channel_id=1, replica_groups=mesh['fsdp'=16,'dp'=8] {'fsdp'}, dimensions={0}, use_global_device_ids=true | all-gather | bytes 4352 | tf_op jit(solution)/shard_map/all_gather | solution.py:103
  65.7 77.6 %all-gather.16.cloned.1.call-done = bf16[2048,6144]{1,0:T(8,128)(2,1)} async-done(((bf16[128,6144]{1,0:T(8,128)(2,1)}), bf16[2048,6144]{1,0:T(8,128)(2,1)}) %all-gather.16.cloned.1.call-update) | async-done | bytes 25165840 | tf_op jit(solution)/shard_map/all_gather | solution.py:104
  162.6 35.5 %all-gather.20.cloned.1.call-done = bf16[2048,2048]{1,0:T(8,128)(2,1)} async-done(((bf16[128,2048]{1,0:T(8,128)(2,1)}), bf16[2048,2048]{1,0:T(8,128)(2,1)}) %all-gather.20.cloned.1.call-update) | async-done | bytes 8388624 | tf_op jit(solution)/shard_map/all_gather | solution.py:106
  205.1 70.5 %all-gather.18.cloned.1.call-done = bf16[1,1024,2048]{1,2,0:T(8,128)(2,1)} async-done(((bf16[1,128,2048]{1,2,0:T(8,128)(2,1)}), bf16[1,1024,2048]{1,2,0:T(8,128)(2,1)}) %all-gather.18.cloned.1.call-update) | async-done | bytes 4194320 | tf_op jit(solution)/shard_map/all_gather | solution.py:150
  282.5 65.3 %all-gather.26.cloned.1.call-done = bf16[1024,2048]{1,0:T(8,128)(2,1)} async-done(((bf16[128,2048]{1,0:T(8,128)(2,1)}), bf16[1024,2048]{1,0:T(8,128)(2,1)}) %all-gather.26.cloned.1.call-update) | async-done | bytes 4194320 | tf_op jit(solution)/shard_map/all_gather | solution.py:153
  357.6 20.7 %copy.84 = bf16[1,1024,2048]{2,0,1:T(2,128)(2,1)} copy(bf16[1,1024,2048]{1,2,0:T(8,128)(2,1)} %bitcast.179) | data formatting | bytes 8388608
  392.1 20.8 %copy.86 = bf16[1,1024,2048]{2,0,1:T(2,128)(2,1)} copy(bf16[1,1024,2048]{1,2,0:T(8,128)(2,1)} %bitcast.182) | data formatting | bytes 8388608
  439.8 29.1 %reduce-scatter.19.cloned.1.call-done = bf16[128,2048]{1,0:T(8,128)(2,1)} async-done(((bf16[1024,2048]{1,0:T(8,128)(2,1)}), bf16[128,2048]{1,0:T(8,128)(2,1)}) %reduce-scatter.19.cloned.1.call-update) | async-done | bytes 524304
  480.2 77.1 %reduce-scatter.21.cloned.1.call-done = bf16[128,2048]{1,0:T(8,128)(2,1)} async-done(((bf16[1024,2048]{1,0:T(8,128)(2,1)}), bf16[128,2048]{1,0:T(8,128)(2,1)}) %reduce-scatter.21.cloned.1.call-update) | async-done | bytes 524304
  593.1 18.9 %all-gather.6 = bf16[16,1,128]{2,1,0:T(2,128)(2,1)S(1)} all-gather(bf16[1,1,128]{2,1,0:T(2,128)(2,1)S(1)} %bitcast.234), channel_id=1, replica_groups=mesh['fsdp'=16,'dp'=8] {'fsdp'}, dimensions={0}, use_global_device_ids=true | all-gather | bytes 4352 | tf_op jit(solution)/shard_map/all_gather | solution.py:109
  628.9 99.6 %all-gather.22.cloned.1.call-done = bf16[2048,8192]{1,0:T(8,128)(2,1)} async-done(((bf16[128,8192]{1,0:T(8,128)(2,1)}), bf16[2048,8192]{1,0:T(8,128)(2,1)}) %all-gather.22.cloned.1.call-update) | async-done | bytes 33554448 | tf_op jit(solution)/shard_map/all_gather | solution.py:110
  728.5 17.2 %convolution_add_fusion = f32[128,8192]{1,0:T(8,128)} fusion(bf16[2048,8192]{1,0:T(8,128)(2,1)} %all-gather.22.cloned.1.call-done, f32[8192]{0:T(1024)S(1)} %bitcast.225, bf16[1,128,2048]{2,1,0:T(8,128)(2,1)S(1)} %copy-done.2, f32[2048]{0:T(1024)S(1)} %bitcast.223, f32[2048]{0:T(1024)S(1)} %bitcast.216, f32[128]{0:T(128)S(1)} %copy-done.25, ...), kind=kOutput, calls=%fused_computation.3 | convolution fusion | flops 4297588736 | bytes 38323200 | tf_op jit(solution)/shard_map/dot_general | solution.py:191
  745.7 23.1 %convolution_convert_fusion.1 = bf16[8192,2048]{1,0:T(8,128)(2,1)} fusion(bf16[1,128,2048]{2,1,0:T(8,128)(2,1)S(1)} %copy-done.4, f32[128,8192]{1,0:T(8,128)} %convolution_add_fusion), kind=kOutput, calls=%fused_computation.1 | convolution fusion | flops 4379901952 | bytes 38273024 | tf_op jit(solution)/shard_map/dot_general | solution.py:214
  769.0 132.8 %all-gather.24.cloned.1.call-done = bf16[8192,2048]{1,0:T(8,128)(2,1)} async-done(((bf16[512,2048]{1,0:T(8,128)(2,1)}), bf16[8192,2048]{1,0:T(8,128)(2,1)}) %all-gather.24.cloned.1.call-update) | async-done | bytes 33554448 | tf_op jit(solution)/shard_map/all_gather | solution.py:112
  901.8 25.0 %fusion.76 = (bf16[8192]{0:T(1024)(128)(2,1)S(1)}, bf16[128,8192]{1,0:T(8,128)(2,1)S(1)}) fusion(f32[128,8192]{1,0:T(8,128)} %convolution_add_fusion, bf16[8192,2048]{1,0:T(8,128)(2,1)} %all-gather.24.cloned.1.call-done, bf16[1,128,2048]{2,1,0:T(8,128)(2,1)S(1)} %copy-done.4), kind=kOutput, calls=%fused_computation.138 | convolution fusion | flops 4371505152 | bytes 40386560 | tf_op jit(solution)/shard_map/dot_general | solution.py:211
  960.5 19.2 %all-gather.8 = bf16[16,1,128]{2,1,0:T(2,128)(2,1)S(1)} all-gather(bf16[1,1,128]{2,1,0:T(2,128)(2,1)S(1)} %bitcast.236), channel_id=1, replica_groups=mesh['fsdp'=16,'dp'=8] {'fsdp'}, dimensions={0}, use_global_device_ids=true | all-gather | bytes 4352 | tf_op jit(solution)/shard_map/all_gather | solution.py:113
  986.2 18.0 %fusion.77 = f32[128,2048]{1,0:T(8,128)} fusion(bf16[128,8192]{1,0:T(8,128)(2,1)S(1)} %get-tuple-element.73, bf16[2048,8192]{1,0:T(8,128)(2,1)} %all-gather.22.cloned.1.call-done), kind=kOutput, calls=%fused_computation.139 | convolution fusion | flops 4294967296 | bytes 36700160 | tf_op jit(solution)/shard_map/dot_general | solution.py:218
  1018.4 99.7 %reduce-scatter.11.cloned.1.call-done = bf16[128,6144]{1,0:T(8,128)(2,1)} async-done(((bf16[2048,6144]{1,0:T(8,128)(2,1)}), bf16[128,6144]{1,0:T(8,128)(2,1)}) %reduce-scatter.11.cloned.1.call-update) | async-done | bytes 1572880 | tf_op jit(solution)/shard_map/reduce_scatter | solution.py:55
  1118.1 183.7 %reduce-scatter.17.cloned.1.call-done = bf16[512,2048]{1,0:T(8,128)(2,1)} async-done(((bf16[8192,2048]{1,0:T(8,128)(2,1)}), bf16[512,2048]{1,0:T(8,128)(2,1)}) %reduce-scatter.17.cloned.1.call-update) | async-done | bytes 2097168 | tf_op jit(solution)/shard_map/reduce_scatter | solution.py:61
  1301.9 183.8 %reduce-scatter.15.cloned.1.call-done = bf16[128,8192]{1,0:T(8,128)(2,1)} async-done(((bf16[2048,8192]{1,0:T(8,128)(2,1)}), bf16[128,8192]{1,0:T(8,128)(2,1)}) %reduce-scatter.15.cloned.1.call-update) | async-done | bytes 2097168 | tf_op jit(solution)/shard_map/reduce_scatter | solution.py:55
  1486.6 57.4 %all-reduce.7 = (bf16[2048]{0:T(1024)(128)(2,1)S(1)}, bf16[2048]{0:T(1024)(128)(2,1)S(1)}, bf16[6144]{0:T(1024)(128)(2,1)S(1)}, bf16[2048]{0:T(1024)(128)(2,1)S(...) all-reduce(bf16[2048]{0:T(1024)(128)(2,1)S(1)} %get-tuple-element.2, ...), channel_id=5, replica_groups=mesh['fsdp'=16,'dp'=8] {'fsdp'}, use_global_device_ids=true, to_apply=%region_12.13.clone | all-reduce | flops 24576 | bytes 98304
  1544.5 26.0 %all-reduce.8 = (bf16[128]{0:T(256)(128)(2,1)S(1)}, bf16[128]{0:T(256)(128)(2,1)S(1)}, bf16[384]{0:T(512)(128)(2,1)S(1)}, bf16[128]{0:T(256)(128)(2,1)S(1)}, bf1...) all-reduce(bf16[128]{0:T(256)(128)(2,1)S(1)} %dynamic-slice.1, ...), channel_id=1, replica_groups=mesh['fsdp'=16,'dp'=8] {'dp'}, use_global_device_ids=true, to_apply=%region_13.14 | all-reduce | flops 1536 | bytes 6144 | tf_op jit(solution)/shard_map/psum | solution.py:69
  1575.2 20.6 %fusion.17 = bf16[1,128,2048]{2,1,0:T(8,128)(2,1)} fusion(f32[128,2048]{1,0:T(8,128)} %fusion.15, bf16[8192,2048]{1,0:T(8,128)(2,1)} %all-gather.24.cloned.1.call-done, f32[2048]{0:T(1024)S(1)} %bitcast.230, f32[128,8192]{1,0:T(8,128)} %convolution_add_fusion), kind=kOutput, calls=%fused_computation.47 | convolution fusion | flops 4363911168 | bytes 39329792 | tf_op jit(solution)/shard_map/dot_general | solution.py:195
  1595.8 43.2 %all-reduce.12.cloned.1.call-done = (bf16[128,6144]{1,0:T(8,128)(2,1)}, bf16[128,2048]{1,0:T(8,128)(2,1)}, bf16[128,8192]{1,0:T(8,128)(2,1)}, bf16[512,2048]{1,0:T(8,128)(2,1)}) async-done(((bf16[128,6144]{1,0:T(8,128)(2,1)}, bf16[128,2048]{1,0:T(8,128)(2,1)}, bf16[128,8192]{1,0:T(8,128)(2,1)}, bf16[512,2048]{1,0:T(8,128)(2,1)}), (bf16[128,6144]{1,0:T(8,128)(2,1)}, bf16[128,2048]{1,0:T(8,128)(2,1)}, ...) | async-done | bytes 6291472 | tf_op jit(solution)/shard_map/psum | solution.py:71
  (203 shorter events, 255.8 us)
Async XLA Ops:
  7.2 136.1 %all-gather.16.cloned.1.call-start = ((), (), s32[]{:S(2)}) async-start(), calls=%async_computation.6 | async-start | bytes 26738688 | tf_op jit(solution)/shard_map/all_gather | solution.py:104
  7.9 190.2 %all-gather.20.cloned.1.call-start = ((), (), s32[]{:S(2)}) async-start(), calls=%async_computation.8 | async-start | bytes 8912896 | tf_op jit(solution)/shard_map/all_gather | solution.py:106
  8.7 267.0 %all-gather.18.cloned.1.call-start = ((), (), s32[]{:S(2)}) async-start(), calls=%async_computation.7 | async-start | bytes 4718592 | tf_op jit(solution)/shard_map/all_gather | solution.py:150
  63.3 90.2 %copy-start.22 = (f32[128]{0:T(128)}, f32[128]{0:T(128)S(1)}, u32[]{:S(2)}) copy-start(f32[128]{0:T(128)S(1)} %broadcast_multiply_fusion) | copy-start | bytes 1540
  64.7 88.9 %copy-start.29 = (f32[128]{0:T(128)}, f32[128]{0:T(128)S(1)}, u32[]{:S(2)}) copy-start(f32[128]{0:T(128)S(1)} %fusion.43) | copy-start | bytes 1540
  64.7 88.9 %copy-start.24 = (f32[128]{0:T(128)}, f32[128]{0:T(128)S(1)}, u32[]{:S(2)}) copy-start(f32[128]{0:T(128)S(1)} %fusion.60) | copy-start | bytes 1540
  65.7 89.4 %copy-start.21 = (f32[128,32]{1,0:T(8,128)}, f32[128,32]{1,0:T(8,128)S(1)}, u32[]{:S(2)}) copy-start(f32[128,32]{1,0:T(8,128)S(1)} %get-tuple-element.66) | copy-start | bytes 49156
  160.1 187.8 %all-gather.26.cloned.1.call-start = ((), (), s32[]{:S(2)}) async-start(), calls=%async_computation.15 | async-start | bytes 4718592 | tf_op jit(solution)/shard_map/all_gather | solution.py:153
  161.1 307.9 %reduce-scatter.19.cloned.1.call-start = ((), (), s32[]{:S(2)}) async-start(), calls=%async_computation.16 | async-start | bytes 4718592
  162.6 113.1 %copy-start.16 = (bf16[128,8,32]{2,0,1:T(8,128)(2,1)S(1)}, bf16[128,8,32]{2,0,1:T(8,128)(2,1)}, u32[]{:S(2)}) copy-start(bf16[128,8,32]{2,0,1:T(8,128)(2,1)} %get-tuple-element.51) | copy-start | bytes 196612
  386.3 170.9 %reduce-scatter.21.cloned.1.call-start = ((), (), s32[]{:S(2)}) async-start(), calls=%async_computation.17 | async-start | bytes 4718592
  421.0 307.5 %all-gather.22.cloned.1.call-start = ((), (), s32[]{:S(2)}) async-start(), calls=%async_computation.9 | async-start | bytes 35651584 | tf_op jit(solution)/shard_map/all_gather | solution.py:110
  421.7 480.1 %all-gather.24.cloned.1.call-start = ((), (), s32[]{:S(2)}) async-start(), calls=%async_computation.10 | async-start | bytes 35651584 | tf_op jit(solution)/shard_map/all_gather | solution.py:112
  422.5 595.9 %reduce-scatter.13.cloned.1.call-start = ((), (), s32[]{:S(2)}) async-start(), calls=%async_computation.12 | async-start | bytes 8912896 | tf_op jit(solution)/shard_map/reduce_scatter | solution.py:61
  433.8 684.4 %reduce-scatter.11.cloned.1.call-start = ((), (), s32[]{:S(2)}) async-start(), calls=%async_computation.11 | async-start | bytes 26738688 | tf_op jit(solution)/shard_map/reduce_scatter | solution.py:55
  475.8 85.0 %copy-start.2 = (bf16[1,128,2048]{2,1,0:T(8,128)(2,1)S(1)}, bf16[1,128,2048]{2,1,0:T(8,128)(2,1)}, u32[]{:S(2)}) copy-start(bf16[1,128,2048]{2,1,0:T(8,128)(2,1)} %param.15) | copy-start | bytes 1572868
  476.6 99.6 %copy-start.12 = (bf16[1,128,8,256]{1,3,2,0:T(8,128)(2,1)}, bf16[1,128,8,256]{1,3,2,0:T(8,128)(2,1)S(1)}, u32[]{:S(2)}) copy-start(bf16[1,128,8,256]{1,3,2,0:T(8,128)(2,1)S(1)} %copy.75) | copy-start | bytes 1572868
  576.2 152.3 %copy-start.23 = (f32[128]{0:T(128)S(1)}, f32[128]{0:T(128)}, u32[]{:S(2)}) copy-start(f32[128]{0:T(128)} %copy-done.22) | copy-start | bytes 1540
  576.2 152.3 %copy-start.25 = (f32[128]{0:T(128)S(1)}, f32[128]{0:T(128)}, u32[]{:S(2)}) copy-start(f32[128]{0:T(128)} %copy-done.24) | copy-start | bytes 1540
  576.3 725.6 %reduce-scatter.17.cloned.1.call-start = ((), (), s32[]{:S(2)}) async-start(), calls=%async_computation.14 | async-start | bytes 35651584 | tf_op jit(solution)/shard_map/reduce_scatter | solution.py:61
  768.8 716.9 %reduce-scatter.15.cloned.1.call-start = ((), (), s32[]{:S(2)}) async-start(), calls=%async_computation.13 | async-start | bytes 35651584 | tf_op jit(solution)/shard_map/reduce_scatter | solution.py:55
  940.9 698.1 %all-reduce.12.cloned.1.call-start = ((), (), s32[]{:S(2)}) async-start(), calls=%async_computation.18 | async-start | bytes 12582912 | tf_op jit(solution)/shard_map/psum | solution.py:71
  1018.3 467.4 %copy-start.3 = (f32[128,2048]{1,0:T(8,128)S(1)}, f32[128,2048]{1,0:T(8,128)}, u32[]{:S(2)}) copy-start(f32[128,2048]{1,0:T(8,128)} %fusion.77) | copy-start | bytes 3145732
  1571.0 78.6 %copy-start.37 = (f32[128]{0:T(128)}, f32[128]{0:T(128)S(1)}, u32[]{:S(2)}) copy-start(f32[128]{0:T(128)S(1)} %convert_element_type.284) | copy-start | bytes 1540
  (27 other events, 296.5 us)
Sparse Core Ops, SparseCore 0:
  9.7 133.5 all-gather.15
  145.0 53.0 all-gather.19
  200.8 74.8 all-gather.17
  278.5 69.3 all-gather.25
  386.4 82.4 reduce-scatter.18
  473.7 83.4 reduce-scatter.20
  558.9 169.5 all-gather.21
  730.2 171.5 all-gather.23
  904.2 71.1 reduce-scatter.12
  977.6 140.4 reduce-scatter.10
  1120.6 181.2 reduce-scatter.16
  1304.2 181.4 reduce-scatter.14
  1488.5 150.4 all-reduce.11
where the time goes:
time: 1660 us
  waiting for transfers between devices  1100 us (66%)
  blocking collectives  223 us (13%)
  matrix products  203 us (12%)
  local copies, waits for them, and re-layouts  80.6 us (5%)
  other arithmetic  30.5 us (2%)
  between operations  16.8 us (1%)
    reduce_scatter x2, waiting for transfers between devices, owner_sums(): lax.psum_scatter(terms[2].astype(jnp.bfloat16), 'fsdp', scatter_dimension...  284 us
    reduce_scatter x2, waiting for transfers between devices, owner_sums(): lax.psum_scatter(terms[4].astype(jnp.bfloat16), 'fsdp', scatter_dimension...  184 us
    all_gather x1, waiting for transfers between devices, body(): lax.all_gather(down_weight, 'fsdp', axis=0, tiled=True)  133 us
    unnamed x15, waiting for transfers between devices  109 us
    all_gather x1, waiting for transfers between devices, body(): lax.all_gather(up_weight, 'fsdp', axis=0, tiled=True)  99.6 us
    all_gather x1, waiting for transfers between devices, body(): lax.all_gather(qkv_weight, 'fsdp', axis=0, tiled=True)  77.6 us
    all_gather x1, waiting for transfers between devices, body(): lax.all_gather(key_vals.reshape(pack_count, shard_len, model_width), 'dp'...  70.5 us
    unnamed x98, local copies, waits for them, and re-layouts  70.1 us
  transfers between devices with their start and end apart: 13, of which 12 were waited for; matrix products, arithmetic and copies ran while one was open for 16% of the time, Pallas kernels for 0%

commit v1 on v0

v1 whole, which is shorter than its diff:
```python
import math

import jax
import jax.numpy as jnp
from jax import lax
from jax.sharding import Mesh, PartitionSpec as P

HEADS = 8
ROTARY = 64
NORM_EPS = 1e-05
MASKED = -1e30
BF = jnp.bfloat16
F32 = jnp.float32
CHIPS = ("x", "y")
COPIES = ("w", "z")


def block_moves():
    moves = []
    for x in range(2):
        for y in range(4):
            for w in range(2):
                for z in range(4):
                    source = ((x * 4 + y) * 2 + w) * 4 + z
                    target = ((w * 4 + (y + z) % 4) * 2 + x) * 4 + y
                    moves.append((source, target))
    return moves


MOVES = block_moves()
BACK = [(target, source) for source, target in MOVES]


def move(block, pairs):
    return lax.ppermute(block, ("x", "y", "w", "z"), pairs)


def swap_core(block):
    return lax.ppermute(block, "c", [(0, 1), (1, 0)])


def dot(a, b, dims):
    return lax.dot_general(a, b, (dims, ((), ())), preferred_element_type=F32)


def rotate(head, cos, sin):
    half = ROTARY // 2
    front, back = head[:, :half], head[:, half:ROTARY]
    return jnp.concatenate(
        [front * cos - back * sin, back * cos + front * sin, head[:, ROTARY:]], axis=1
    )


def core_pair(own, other, core, axis):
    return jnp.where(core == 0, jnp.stack([own, other], axis), jnp.stack([other, own], axis))


def core_sum(both, core, axis):
    keep = lax.dynamic_index_in_dim(both, core, axis, keepdims=False)
    give = lax.dynamic_index_in_dim(both, 1 - core, axis, keepdims=False)
    got = swap_core(give)
    return (keep.astype(F32) + got.astype(F32)).astype(BF)


def body(
    tokens, segment_ids, out_cotangent, ln1_gain, ln1_bias, qkv_weight, qkv_bias, out_weight, out_bias,
    ln2_gain, ln2_bias, up_weight, up_bias, down_weight, down_bias,
):
    _, shard, width = tokens.shape
    head_dim = width // HEADS
    ff = up_weight.shape[1]
    ff_part = ff // 8
    core = lax.axis_index("c")
    chip = lax.axis_index("x") * 4 + lax.axis_index("y")
    scale = head_dim ** -0.5

    x_own = move(tokens[0], MOVES)
    x_all = lax.all_gather(x_own, CHIPS, axis=0, tiled=True)
    ids = move(segment_ids, MOVES)[0]

    small = [ln1_gain, ln1_bias, out_bias, ln2_gain, ln2_bias, down_bias, qkv_bias, up_bias]
    small_all = lax.all_gather(jnp.concatenate(small), ("x", "y", "c"), axis=0)
    cut = width // 16
    gain_one, bias_one, b_out, gain_two, bias_two, b_down = (
        small_all[:, i * cut : (i + 1) * cut].reshape(width).astype(F32) for i in range(6)
    )
    b_qkv = small_all[:, 6 * cut : 9 * cut].reshape(3, HEADS, head_dim)
    b_qkv = lax.dynamic_index_in_dim(b_qkv, chip, 1, keepdims=False).reshape(3 * head_dim).astype(F32)
    b_up = small_all[:, 9 * cut :].reshape(8, ff_part)
    b_up = lax.dynamic_index_in_dim(b_up, chip, 0, keepdims=False).astype(F32)

    rows = qkv_weight.shape[0]
    q_cols = qkv_weight.reshape(rows, 3, HEADS, head_dim).transpose(2, 0, 1, 3).reshape(HEADS, rows, 3 * head_dim)
    q_half = lax.all_to_all(q_cols, CHIPS, 0, 0, tiled=True)
    w_qkv = core_pair(q_half, swap_core(q_half), core, 1).reshape(width, 3 * head_dim)
    u_cols = up_weight.reshape(rows, 8, ff_part).transpose(1, 0, 2)
    u_half = lax.all_to_all(u_cols, CHIPS, 0, 0, tiled=True)
    w_up = core_pair(u_half, swap_core(u_half), core, 1).reshape(width, ff_part)
    w_down = core_pair(down_weight, swap_core(down_weight), core, 0).reshape(ff_part, width)
    w_out = core_pair(out_weight, swap_core(out_weight), core, 0).reshape(head_dim, width)
    w_rows = jnp.concatenate([w_down, w_out], axis=0)

    g_own = move(out_cotangent[0], MOVES)
    g_all = lax.all_gather(g_own, CHIPS, axis=0, tiled=True)

    slot = jnp.arange(8, dtype=jnp.int32)
    block = (slot // 4) * 4 + (slot % 4 - lax.axis_index("z") + 4) % 4
    places = (block[:, None] * shard + jnp.arange(shard, dtype=jnp.int32)[None, :]).reshape(8 * shard)
    freqs = jnp.exp(jnp.arange(ROTARY // 2, dtype=F32) * (-2.0 * math.log(10000.0) / ROTARY))
    angles = places.astype(F32)[:, None] * freqs[None, :]
    cos, sin = jnp.cos(angles), jnp.sin(angles)
    ids_slot = jnp.take(ids.reshape(8, shard), block, axis=0).reshape(8 * shard)

    xf = x_all.astype(F32)
    center = xf - jnp.mean(xf, axis=-1, keepdims=True)
    rstd = lax.rsqrt(jnp.mean(center * center, axis=-1, keepdims=True) + NORM_EPS)
    xhat = center * rstd
    h1 = (xhat * gain_one + bias_one).astype(BF)
    h2 = (xhat * gain_two + bias_two).astype(BF)
    mixed = dot(h1, w_qkv, ((1,), (0,))) + b_qkv
    query = rotate(mixed[:, :head_dim], cos, sin).astype(BF)
    key = rotate(mixed[:, head_dim : 2 * head_dim], cos, sin).astype(BF)
    value = mixed[:, 2 * head_dim :].astype(BF)
    same = places[:, None] == places[None, :]
    allowed = (
        (ids_slot[:, None] == ids_slot[None, :]) & (ids_slot[None, :] >= 0) & (places[None, :] <= places[:, None])
    ) | same
    scores = jnp.where(allowed, dot(query, key, ((1,), (1,))) * scale, MASKED)
    expo = jnp.exp(scores - jnp.max(scores, axis=-1, keepdims=True))
    prob = expo / jnp.sum(expo, axis=-1, keepdims=True)
    prob_low = prob.astype(BF)
    attended = dot(prob_low, value, ((1,), (0,))).astype(BF)
    pre = dot(h2, w_up, ((1,), (0,))) + b_up
    act = jax.nn.gelu(pre, approximate=False).astype(BF)
    branches = jnp.concatenate([act, attended], axis=1)
    out_part = dot(branches, w_rows, ((1,), (0,))).astype(BF)
    out_sum = lax.psum_scatter(out_part, CHIPS, scatter_dimension=0, tiled=True)
    x_rows = x_own.astype(F32)
    layer_output = move((x_rows + out_sum.astype(F32) + (b_out + b_down)).astype(BF), BACK)

    g_branches = dot(g_all, w_rows, ((1,), (1,)))
    _, gelu_back = jax.vjp(lambda v: jax.nn.gelu(v, approximate=False), pre)
    g_pre = gelu_back(g_branches[:, :ff_part])[0].astype(BF)
    g_att = g_branches[:, ff_part:].astype(BF)
    grad_rows = dot(branches, g_all, ((0,), (0,))).astype(BF)
    grad_up = dot(h2, g_pre, ((0,), (0,))).astype(BF)
    grad_up_bias = jnp.sum(g_pre.astype(F32), axis=0)
    e2 = dot(g_pre, w_up, ((1,), (1,)))
    g_value = dot(prob_low, g_att, ((0,), (0,)))
    g_prob = dot(g_att, value, ((1,), (1,)))
    inner = jnp.sum(prob * g_prob, axis=-1, keepdims=True)
    g_scores = (prob * (g_prob - inner)).astype(BF)
    g_query = rotate(dot(g_scores, key, ((1,), (0,))) * scale, cos, -sin)
    g_key = rotate(dot(g_scores, query, ((0,), (0,))) * scale, cos, -sin)
    g_mixed = jnp.concatenate([g_query, g_key, g_value], axis=1).astype(BF)
    grad_qkv = dot(h1, g_mixed, ((0,), (0,))).astype(BF)
    grad_qkv_bias = jnp.sum(g_mixed.astype(F32), axis=0)
    e1 = dot(g_mixed, w_qkv, ((1,), (1,)))
    e_part = (e1 * gain_one + e2 * gain_two).astype(BF)
    e_own = lax.psum_scatter(e_part, CHIPS, scatter_dimension=0, tiled=True).astype(F32)
    center_own = x_rows - jnp.mean(x_rows, axis=-1, keepdims=True)
    rstd_own = lax.rsqrt(jnp.mean(center_own * center_own, axis=-1, keepdims=True) + NORM_EPS)
    xhat_own = center_own * rstd_own
    grad_x = rstd_own * (
        e_own - jnp.mean(e_own, axis=-1, keepdims=True) - xhat_own * jnp.mean(e_own * xhat_own, axis=-1, keepdims=True)
    )
    input_grad = move((g_own.astype(F32) + grad_x).astype(BF), BACK)

    def at_chip(vec, parts):
        full = jnp.zeros((parts, 8, vec.shape[0] // parts), F32)
        return lax.dynamic_update_slice_in_dim(full, vec.reshape(parts, 1, -1), chip, 1).reshape(-1)

    norms = [
        jnp.sum(e1 * xhat, axis=0), jnp.sum(e1, axis=0), jnp.sum(e2 * xhat, axis=0), jnp.sum(e2, axis=0),
        jnp.sum(g_own.astype(F32), axis=0),
    ]
    sums = jnp.concatenate(norms + [at_chip(grad_qkv_bias, 3), at_chip(grad_up_bias, 1)])
    sums = lax.psum(sums, ("x", "y", "c", "w", "z"))
    owner = chip * 2 + core

    def own_part(start, size):
        step = size // 16
        return lax.dynamic_slice_in_dim(sums, start + owner * step, step)

    grad_g1, grad_b1, grad_g2, grad_b2, grad_ob = (own_part(i * width, width) for i in range(5))
    grad_qb = own_part(5 * width, 3 * width)
    grad_ub = own_part(8 * width, ff)

    down_own = core_sum(grad_rows[:ff_part].reshape(2, ff_part // 2, width), core, 0)
    out_own = core_sum(grad_rows[ff_part:].reshape(2, head_dim // 2, width), core, 0)
    grad_down, grad_out = lax.psum((down_own, out_own), COPIES)

    def by_columns(grad):
        cols = grad.shape[1]
        own = core_sum(grad.reshape(8, 2, rows, cols), core, 1)
        own = own.transpose(1, 0, 2)
        own = lax.psum_scatter(own, COPIES, scatter_dimension=0, tiled=True)
        own = lax.all_to_all(own, CHIPS, 1, 1, tiled=True)
        return lax.all_gather(own, COPIES, axis=0, tiled=True)

    grad_up = by_columns(grad_up).reshape(rows, ff)
    grad_qkv = by_columns(grad_qkv).reshape(rows, HEADS, 3, head_dim).transpose(0, 2, 1, 3).reshape(rows, 3 * width)

    return (
        layer_output[None], input_grad[None], grad_g1, grad_b1, grad_qkv.astype(F32), grad_qb, grad_out.astype(F32),
        grad_ob, grad_g2, grad_b2, grad_up.astype(F32), grad_ub, grad_down.astype(F32), grad_ob,
    )


def solution(mesh):
    fine = Mesh(mesh.devices.reshape(2, 4, 2, 2, 4), ("x", "y", "c", "w", "z"))
    by_owner, by_place = ("x", "y", "c"), ("w", "z")
    act, vec, mat = P(by_owner, by_place, None), P(by_owner), P(by_owner, None)
    return jax.shard_map(
        body,
        mesh=fine,
        in_specs=(act, mat, act, vec, vec, mat, vec, mat, vec, vec, vec, mat, vec, mat, vec),
        out_specs=(act, act, vec, vec, mat, vec, mat, vec, vec, vec, mat, vec, mat, vec),
        check_vma=False,
    )
```

time: 1660 us -> 910 us (0.55)
  waiting for transfers between devices: 1100 us -> 611 us
  blocking collectives: 223 us -> 30.3 us
  matrix products: 203 us -> 85.5 us
  starting transfers between devices: 1.55 us -> 59.6 us
  local copies, waits for them, and re-layouts: 80.6 us -> 46.7 us
  other arithmetic: 30.5 us -> 54.5 us
    all_gather x6 -> x4, waiting for transfers between devices: 481 us -> 94.2 us  [the longest x2 94.2 us: by_columns(): return lax.all_gather(own, COPIES, axis=0, tiled=True)]
    reduce_scatter x4, waiting for transfers between devices: 467 us -> 180 us  [the longest x2 79.1 us: by_columns(): own = lax.psum_scatter(own, COPIES, scatter_dimension=0, tiled=True)]
    psum x1 -> x2, waiting for transfers between devices: 43.2 us -> 264 us  [the longest x1 138 us: body(): sums = lax.psum(sums, ('x', 'y', 'c', 'w', 'z'))]
    all_gather x8 -> x1, blocking collectives: 140 us -> 20.5 us  [body(): small_all = lax.all_gather(jnp.concatenate(small), ('x', 'y', 'c'), axis=0)]
    dot_general x18 -> x15, matrix products: 203 us -> 85.5 us  [dot(): return lax.dot_general(a, b, (dims, ((), ())), preferred_element_type=F32)]
    unnamed x15 -> x10, waiting for transfers between devices: 109 us -> 0.16 us
    ppermute x0 -> x13, waiting for transfers between devices: none -> 72.6 us  [the longest x5 64.5 us: move(): return lax.ppermute(block, ('x', 'y', 'w', 'z'), pairs)]
    unnamed x1 -> x0, blocking collectives: 57.4 us -> none
  transfers between devices with their start and end apart: 13 -> 26, of which waited for: 12 -> 12; matrix products, arithmetic and copies ran while one was open for 16% -> 16% of each run, Pallas kernels for 0% -> 0%
where the time goes in v1:
time: 910 us; the launch traced here: 903 us
  waiting for transfers between devices  611 us (67%)
  matrix products  85.5 us (9%)
  starting transfers between devices  59.6 us (7%)
  other arithmetic  54.5 us (6%)
  local copies, waits for them, and re-layouts  46.7 us (5%)
  blocking collectives  30.3 us (3%)
  between operations  15.7 us (2%)
    psum x1, waiting for transfers between devices, body(): sums = lax.psum(sums, ('x', 'y', 'c', 'w', 'z'))  138 us
    psum x1, waiting for transfers between devices, body(): grad_down, grad_out = lax.psum((down_own, out_own), COPIES)  127 us
    all_gather x2, waiting for transfers between devices, by_columns(): return lax.all_gather(own, COPIES, axis=0, tiled=True)  94.2 us
    dot_general x15, matrix products, dot(): return lax.dot_general(a, b, (dims, ((), ())), preferred_element_type=F32)  85.5 us
    reduce_scatter x2, waiting for transfers between devices, by_columns(): own = lax.psum_scatter(own, COPIES, scatter_dimension=0, tiled=True)  79.1 us
    ppermute x5, waiting for transfers between devices, move(): return lax.ppermute(block, ('x', 'y', 'w', 'z'), pairs)  64.5 us
    reduce_scatter x1, waiting for transfers between devices, body(): out_sum = lax.psum_scatter(out_part, CHIPS, scatter_dimension=0, tiled=True)  53.4 us
    reduce_scatter x1, waiting for transfers between devices, body(): lax.psum_scatter(e_part, CHIPS, scatter_dimension=0, tiled=True).astype(F32)  47.2 us
  transfers between devices with their start and end apart: 26, of which 12 were waited for; matrix products, arithmetic and copies ran while one was open for 16% of the time, Pallas kernels for 0%

profile of v1, /device:TPU:8, one launch (start us, length us, event | category | flops | bytes accessed | tf_op | source)
XLA Modules:
  0.0 903.3 jit_solution(14791005468657810709)
XLA Ops:
  11.1 12.8 %collective-permute-done = bf16[128,2048]{1,0:T(8,128)(2,1)S(1)} collective-permute-done((bf16[128,2048]{1,0:T(8,128)(2,1)}, bf16[128,2048]{1,0:T(8,128)(2,1)S(1)}, u32[]{:S(2)}, u32[]{:S(2)}) %collective-permute-start) | collective-permute-done | bytes 524320 | tf_op jit(solution)/shard_map/ppermute | solution.py:35
  28.9 9.8 %all-to-all-start = ((bf16[8,128,1024]{1,2,0:T(8,128)(2,1)}), bf16[8,128,1024]{1,2,0:T(8,128)(2,1)}, u32[]{:S(2)}, u32[]{:S(2)}) async-start(bf16[8,128,1024]{1,2,0:T(8,128)(2,1)} %bitcast.4), calls=%async_computation | async-start | bytes 4194304 | tf_op jit(solution)/shard_map/all_to_all | solution.py:97
  40.9 51.6 %collective-permute-done.7 = bf16[128,2048]{1,0:T(8,128)(2,1)S(1)} collective-permute-done((bf16[128,2048]{1,0:T(8,128)(2,1)S(1)}, bf16[128,2048]{1,0:T(8,128)(2,1)S(1)}, u32[]{:S(2)}, u32[]{:S(2)}) %collective-permute-start.7) | collective-permute-done | bytes 524320 | tf_op jit(solution)/shard_map/ppermute | solution.py:35
  95.6 24.9 %all-to-all-start.1 = ((bf16[8,128,768]{1,2,0:T(8,128)(2,1)}), bf16[8,128,768]{1,2,0:T(8,128)(2,1)S(1)}, u32[]{:S(2)}, u32[]{:S(2)}) async-start(bf16[8,128,768]{1,2,0:T(8,128)(2,1)} %bitcast.17), calls=%async_computation.1 | async-start | bytes 3145728 | tf_op jit(solution)/shard_map/all_to_all | solution.py:94
  124.8 20.5 %all-gather.1 = bf16[16,1,1664]{2,1,0:T(2,128)(2,1)S(1)} all-gather(bf16[1,1,1664]{2,1,0:T(2,128)(2,1)S(1)} %reshape.420), channel_id=2, replica_groups=mesh['x'=2,'y'=4,'c'=2,'w'=2,'z'=4] {'x','y','c'}, dimensions={0}, use_global_device_ids=true | all-gather | bytes 56576 | tf_op jit(solution)/shard_map/all_gather | solution.py:82
  151.0 5.9 maximum_select_fusion.1
  164.2 5.8 maximum_select_fusion
  169.9 6.5 copy.48
  191.0 9.6 %convolution_bitcast_fusion = f32[1024,1280]{1,0:T(8,128)S(1)} fusion(bf16[1024,2048]{1,0:T(8,128)(2,1)} %all-gather.9.cloned.1.call-done, bf16[256,2048]{1,0:T(8,128)(2,1)} %bitcast.139, bf16[1024,2048]{1,0:T(8,128)(2,1)} %bitcast.126), kind=kOutput, calls=%fused_computation.20 | convolution fusion | flops 5379194880 | bytes 14680064 | tf_op jit(solution)/shard_map/dot_general | solution.py:43
  217.5 16.7 %convert_reduce_fusion.1 = (f32[1024]{0:T(1024)S(1)}, bf16[1024,1024]{1,0:T(8,128)(2,1)}, f32[1024,1024]{1,0:T(8,128)}, f32[1024,1024]{1,0:T(8,128)}) fusion(f32[1024,1280]{1,0:T(8,128)S(1)} %convolution_bitcast_fusion, f32[1024]{0:T(1024)S(1)} %bitcast.149, bf16[2048,1024]{1,0:T(8,128)(2,1)S(1)} %bitcast.128, bf16[1024,2048]{1,0:T(8,128)(2,1)S(1)} %copy-done.1, ...), kind=kOutput, calls=%fused_computation.29 | convolution fusion | flops 4386192384 | bytes 23101440 | tf_op jit(solution)/shard_map/dot_general | solution.py:43
  236.4 7.8 convolution_convert_fusion.2
  251.3 7.2 fusion.119
  258.6 10.6 %fusion.112 = (f32[2048]{0:T(1024)S(1)}, f32[2048]{0:T(1024)S(1)}, bf16[1024,2048]{1,0:T(8,128)(2,1)}, f32[2048]{0:T(1024)S(1)}, f32[2048]{0:T(1024)S(1)}) fusion(f32[1024]{0:T(1024)S(1)} %copy-done.45, f32[1024]{0:T(1024)S(1)} %copy-done.35, bf16[1024,2048]{1,0:T(8,128)(2,1)S(1)} %copy-done.2, f32[2048]{0:T(1024)S(1)} %copy-done.38, ...), kind=kOutput, calls=%fused_computation.217 | convolution fusion | flops 4322222080 | bytes 23126016 | tf_op jit(solution)/shard_map/dot_general | solution.py:43
  276.8 7.1 convolution_convert_fusion.1
  284.2 8.3 convolution_convert_fusion
  301.3 14.5 %reduce-scatter.9.cloned.1.call-done = bf16[16,8,768]{2,1,0:T(8,128)(2,1)} async-done(((bf16[128,8,768]{2,1,0:T(8,128)(2,1)}), bf16[16,8,768]{2,1,0:T(8,128)(2,1)}) %reduce-scatter.9.cloned.1.call-update) | async-done | bytes 196624 | tf_op jit(solution)/shard_map/reduce_scatter | solution.py:197
  316.8 9.9 %all_to_all.20 = bf16[16,8,768]{2,0,1:T(8,128)(2,1)S(1)} all-to-all(bf16[16,8,768]{2,0,1:T(8,128)(2,1)S(1)} %copy.55), channel_id=1, replica_groups=mesh['x'=2,'y'=4,'c'=2,'w'=2,'z'=4] {'x','y'}, dimensions={1} | all-to-all | bytes 393216 | tf_op jit(solution)/shard_map/all_to_all | solution.py:198
  329.1 64.6 %reduce-scatter.11.cloned.1.call-done = bf16[16,8,1024]{2,0,1:T(8,128)(2,1)} async-done(((bf16[128,8,1024]{2,0,1:T(8,128)(2,1)}), bf16[16,8,1024]{2,0,1:T(8,128)(2,1)}) %reduce-scatter.11.cloned.1.call-update) | async-done | bytes 262160 | tf_op jit(solution)/shard_map/reduce_scatter | solution.py:197
  398.6 47.2 %reduce-scatter.7.cloned.1.call-done = bf16[128,2048]{1,0:T(8,128)(2,1)} async-done(((bf16[1024,2048]{1,0:T(8,128)(2,1)}), bf16[128,2048]{1,0:T(8,128)(2,1)}) %reduce-scatter.7.cloned.1.call-update) | async-done | bytes 524304 | tf_op jit(solution)/shard_map/reduce_scatter | solution.py:160
  447.3 53.4 %reduce-scatter.5.cloned.1.call-done = bf16[128,2048]{1,0:T(8,128)(2,1)} async-done(((bf16[1024,2048]{1,0:T(8,128)(2,1)}), bf16[128,2048]{1,0:T(8,128)(2,1)}) %reduce-scatter.5.cloned.1.call-update) | async-done | bytes 524304 | tf_op jit(solution)/shard_map/reduce_scatter | solution.py:137
  513.6 126.8 %all-reduce.6.cloned.1.call-done = (bf16[128,2048]{1,0:T(8,128)(2,1)}, bf16[512,2048]{1,0:T(8,128)(2,1)}) async-done(((bf16[128,2048]{1,0:T(8,128)(2,1)}, bf16[512,2048]{1,0:T(8,128)(2,1)}), (bf16[128,2048]{1,0:T(8,128)(2,1)}, bf16[512,2048]{1,0:T(8,128)(2,1)})) %all-reduce.6.cloned.1.call-update) | async-done | bytes 2621456 | tf_op jit(solution)/shard_map/psum | solution.py:191
  646.6 44.2 %all-gather.11.cloned.1.call-done = bf16[128,8,768]{2,1,0:T(8,128)(2,1)} async-done(((bf16[16,8,768]{2,1,0:T(8,128)(2,1)}), bf16[128,8,768]{2,1,0:T(8,128)(2,1)}) %all-gather.11.cloned.1.call-update) | async-done | bytes 1572880 | tf_op jit(solution)/shard_map/all_gather | solution.py:199
  695.8 137.6 %all-reduce.4.cloned.1.call-done = f32[24576]{0:T(1024)} async-done(((f32[24576]{0:T(1024)}), f32[24576]{0:T(1024)}) %all-reduce.4.cloned.1.call-update) | async-done | bytes 98320 | tf_op jit(solution)/shard_map/psum | solution.py:178
  837.4 50.0 %all-gather.13.cloned.1.call-done = bf16[128,8,1024]{2,0,1:T(8,128)(2,1)} async-done(((bf16[16,8,1024]{2,0,1:T(8,128)(2,1)}), bf16[128,8,1024]{2,0,1:T(8,128)(2,1)}) %all-gather.13.cloned.1.call-update) | async-done | bytes 2097168 | tf_op jit(solution)/shard_map/all_gather | solution.py:199
  (275 shorter events, 134.3 us)
Async XLA Ops:
  7.2 169.2 %all-gather.7.cloned.1.call-start = ((), (), s32[]{:S(2)}) async-start(), calls=%async_computation.8 | async-start | bytes 4718592 | tf_op jit(solution)/shard_map/all_gather | solution.py:78
  7.2 16.7 %collective-permute-start = (bf16[128,2048]{1,0:T(8,128)(2,1)}, bf16[128,2048]{1,0:T(8,128)(2,1)S(1)}, u32[]{:S(2)}, u32[]{:S(2)}) collective-permute-start(bf16[128,2048]{1,0:T(8,128)(2,1)} %bitcast.152), channel_id=1, source_target_pairs={{0,0},{1,16},{2,32},{3,48},{4,64},{5,80},{6,96},{7,112},{16,17},{1... | collective-permute-start | bytes 1572872 | tf_op jit(solution)/shard_map/ppermute | solution.py:35
  28.9 66.6 %all-to-all-start = ((bf16[8,128,1024]{1,2,0:T(8,128)(2,1)}), bf16[8,128,1024]{1,2,0:T(8,128)(2,1)}, u32[]{:S(2)}, u32[]{:S(2)}) async-start(bf16[8,128,1024]{1,2,0:T(8,128)(2,1)} %bitcast.4), calls=%async_computation | async-start | bytes 4194304 | tf_op jit(solution)/shard_map/all_to_all | solution.py:97
  38.7 152.3 %all-gather.9.cloned.1.call-start = ((), (), s32[]{:S(2)}) async-start(), calls=%async_computation.10 | async-start | bytes 4718592 | tf_op jit(solution)/shard_map/all_gather | solution.py:104
  38.7 53.8 %collective-permute-start.7 = (bf16[128,2048]{1,0:T(8,128)(2,1)S(1)}, bf16[128,2048]{1,0:T(8,128)(2,1)S(1)}, u32[]{:S(2)}, u32[]{:S(2)}) collective-permute-start(bf16[128,2048]{1,0:T(8,128)(2,1)S(1)} %bitcast.153), channel_id=1, source_target_pairs={{0,0},{1,16},{2,32},{3,48},{4,64},{5,80},{6,96},{7,112},{16,17},{1... | collective-permute-start | bytes 1572872 | tf_op jit(solution)/shard_map/ppermute | solution.py:35
  95.6 50.2 %all-to-all-start.1 = ((bf16[8,128,768]{1,2,0:T(8,128)(2,1)}), bf16[8,128,768]{1,2,0:T(8,128)(2,1)S(1)}, u32[]{:S(2)}, u32[]{:S(2)}) async-start(bf16[8,128,768]{1,2,0:T(8,128)(2,1)} %bitcast.17), calls=%async_computation.1 | async-start | bytes 3145728 | tf_op jit(solution)/shard_map/all_to_all | solution.py:94
  120.5 195.3 %reduce-scatter.9.cloned.1.call-start = ((), (), s32[]{:S(2)}) async-start(), calls=%async_computation.13 | async-start | bytes 1769472 | tf_op jit(solution)/shard_map/reduce_scatter | solution.py:197
  120.5 30.5 %collective-permute-start.4 = (bf16[512,2048]{1,0:T(8,128)(2,1)}, bf16[512,2048]{1,0:T(8,128)(2,1)}, u32[]{:S(2)}, u32[]{:S(2)}) collective-permute-start(bf16[512,2048]{1,0:T(8,128)(2,1)} %param.28), channel_id=1, source_target_pairs={{0,8},{8,0},{1,9},{9,1},{2,10},{10,2},{3,11},{11,3},{4,12},{12,4},... | collective-permute-start | bytes 6291464 | tf_op jit(solution)/shard_map/ppermute | solution.py:39
  120.5 26.5 %collective-permute-start.2 = (s32[1,1024]{1,0:T(1,128)S(1)}, s32[1,1024]{1,0:T(1,128)S(1)}, u32[]{:S(2)}, u32[]{:S(2)}) collective-permute-start(s32[1,1024]{1,0:T(1,128)S(1)} %copy-done.58), channel_id=1, source_target_pairs={{0,0},{1,16},{2,32},{3,48},{4,64},{5,80},{6,96},{7,112},{16,17},{1... | collective-permute-start | bytes 12296 | tf_op jit(solution)/shard_map/ppermute | solution.py:35
  122.5 25.8 %collective-permute-start.5 = (bf16[128,2048]{1,0:T(8,128)(2,1)}, bf16[128,2048]{1,0:T(8,128)(2,1)}, u32[]{:S(2)}, u32[]{:S(2)}) collective-permute-start(bf16[128,2048]{1,0:T(8,128)(2,1)} %param.22), channel_id=1, source_target_pairs={{0,8},{8,0},{1,9},{9,1},{2,10},{10,2},{3,11},{11,3},{4,12},{12,4},... | collective-permute-start | bytes 1572872 | tf_op jit(solution)/shard_map/ppermute | solution.py:39
  145.3 18.9 %collective-permute-start.1 = (bf16[8,128,1024]{1,2,0:T(8,128)(2,1)}, bf16[8,128,1024]{1,2,0:T(8,128)(2,1)}, u32[]{:S(2)}, u32[]{:S(2)}) collective-permute-start(bf16[8,128,1024]{1,2,0:T(8,128)(2,1)} %all-to-all-done), channel_id=1, source_target_pairs={{0,8},{8,0},{1,9},{9,1},{2,10},{10,2},{3,11},{11,3},{4,12},{12,4},... | collective-permute-start | bytes 6291464 | tf_op jit(solution)/shard_map/ppermute | solution.py:39
  145.8 11.1 %collective-permute-start.3 = (bf16[8,128,768]{1,2,0:T(8,128)(2,1)S(1)}, bf16[8,128,768]{1,2,0:T(8,128)(2,1)S(1)}, u32[]{:S(2)}, u32[]{:S(2)}) collective-permute-start(bf16[8,128,768]{1,2,0:T(8,128)(2,1)S(1)} %all-to-all-done.1), channel_id=1, source_target_pairs={{0,8},{8,0},{1,9},{9,1},{2,10},{10,2},{3,11},{11,3},{4,12},{12,4},... | collective-permute-start | bytes 4718600 | tf_op jit(solution)/shard_map/ppermute | solution.py:39
  216.5 17.7 %collective-permute-start.9 = (bf16[8,128,768]{2,0,1:T(8,128)(2,1)S(1)}, bf16[8,128,768]{2,0,1:T(8,128)(2,1)S(1)}, u32[]{:S(2)}, u32[]{:S(2)}) collective-permute-start(bf16[8,128,768]{2,0,1:T(8,128)(2,1)S(1)} %bitcast.137), channel_id=1, source_target_pairs={{0,8},{8,0},{1,9},{9,1},{2,10},{10,2},{3,11},{11,3},{4,12},{12,4},... | collective-permute-start | bytes 4718600 | tf_op jit(solution)/shard_map/ppermute | solution.py:39
  236.3 157.4 %reduce-scatter.11.cloned.1.call-start = ((), (), s32[]{:S(2)}) async-start(), calls=%async_computation.15 | async-start | bytes 2359296 | tf_op jit(solution)/shard_map/reduce_scatter | solution.py:197
  251.2 194.6 %reduce-scatter.7.cloned.1.call-start = ((), (), s32[]{:S(2)}) async-start(), calls=%async_computation.11 | async-start | bytes 4718592 | tf_op jit(solution)/shard_map/reduce_scatter | solution.py:160
  269.2 231.5 %reduce-scatter.5.cloned.1.call-start = ((), (), s32[]{:S(2)}) async-start(), calls=%async_computation.9 | async-start | bytes 4718592 | tf_op jit(solution)/shard_map/reduce_scatter | solution.py:137
  283.9 356.4 %all-reduce.6.cloned.1.call-start = ((), (), s32[]{:S(2)}) async-start(), calls=%async_computation.17 | async-start | bytes 5242880 | tf_op jit(solution)/shard_map/psum | solution.py:191
  293.2 5.9 collective-permute-start.12
  301.3 389.5 %all-gather.11.cloned.1.call-start = ((), (), s32[]{:S(2)}) async-start(), calls=%async_computation.14 | async-start | bytes 1769472 | tf_op jit(solution)/shard_map/all_gather | solution.py:199
  393.8 110.5 %all-to-all-start.3 = ((bf16[16,8,1024]{2,0,1:T(8,128)(2,1)}), bf16[16,8,1024]{2,0,1:T(8,128)(2,1)S(1)}, u32[]{:S(2)}, u32[]{:S(2)}) async-start(bf16[16,8,1024]{2,0,1:T(8,128)(2,1)} %reduce-scatter.11.cloned.1.call-done), calls=%async_computation.7 | async-start | bytes 524288 | tf_op jit(solution)/shard_map/all_to_all | solution.py:198
  398.6 434.8 %all-reduce.4.cloned.1.call-start = ((), (), s32[]{:S(2)}) async-start(), calls=%async_computation.12 | async-start | bytes 196608 | tf_op jit(solution)/shard_map/psum | solution.py:178
  504.2 383.1 %all-gather.13.cloned.1.call-start = ((), (), s32[]{:S(2)}) async-start(), calls=%async_computation.16 | async-start | bytes 2359296 | tf_op jit(solution)/shard_map/all_gather | solution.py:199
  505.0 332.4 %collective-permute-start.8 = (bf16[128,2048]{1,0:T(8,128)(2,1)}, bf16[128,2048]{1,0:T(8,128)(2,1)}, u32[]{:S(2)}, u32[]{:S(2)}) collective-permute-start(bf16[128,2048]{1,0:T(8,128)(2,1)} %get-tuple-element.67), channel_id=1, source_target_pairs={{0,0},{16,1},{32,2},{48,3},{64,4},{80,5},{96,6},{112,7},{17,16},{3... | collective-permute-start | bytes 1572872 | tf_op jit(solution)/shard_map/ppermute | solution.py:35
  510.6 326.7 %collective-permute-start.6 = (bf16[128,2048]{1,0:T(8,128)(2,1)}, bf16[128,2048]{1,0:T(8,128)(2,1)}, u32[]{:S(2)}, u32[]{:S(2)}) collective-permute-start(bf16[128,2048]{1,0:T(8,128)(2,1)} %get-tuple-element.68), channel_id=1, source_target_pairs={{0,0},{16,1},{32,2},{48,3},{64,4},{80,5},{96,6},{112,7},{17,16},{3... | collective-permute-start | bytes 1572872 | tf_op jit(solution)/shard_map/ppermute | solution.py:35
  (62 other events, 926.7 us)
Sparse Core Ops, SparseCore 0:
  24.8 82.7 all-gather.6
  109.8 78.1 all-gather.8
  236.4 79.3 reduce-scatter.8
  319.8 73.8 reduce-scatter.10
  396.1 49.6 reduce-scatter.6
  448.8 51.8 reduce-scatter.4
  504.0 136.2 all-reduce.5
  642.9 47.8 all-gather.10
  696.2 137.1 all-reduce.3
  836.1 51.2 all-gather.12

commit v2 on v1

v2 whole, which is shorter than its diff:
```python
import math

import jax
import jax.numpy as jnp
from jax import lax
from jax.experimental import pallas as pl
from jax.experimental.pallas import tpu as pltpu
from jax.sharding import Mesh, PartitionSpec as P

HEADS = 8
ROTARY = 64
NORM_EPS = 1e-05
MASKED = -1e30
BF = jnp.bfloat16
F32 = jnp.float32
LANES = 128
TILE = 256
VMEM_BYTES = 56 * 1024 * 1024
AXES = ("x", "y", "c", "w", "z")
SIZES = {"x": 2, "y": 4, "c": 2, "w": 2, "z": 4}
CHIPS = ("x", "y")


def pairs_of(axes, target):
    pairs = []
    total = math.prod(SIZES[a] for a in axes)
    for source in range(total):
        rest, at = source, {}
        for a in reversed(axes):
            at[a] = rest % SIZES[a]
            rest //= SIZES[a]
        to, number = {**at, **target(at)}, 0
        for a in axes:
            number = number * SIZES[a] + to[a] % SIZES[a]
        pairs.append((source, number))
    return pairs


def send(block, axes, target):
    return lax.ppermute(block, axes, pairs_of(axes, target))


def place_target(at):
    if at["c"] == 0:
        return {"x": at["w"], "y": at["y"] + at["z"], "w": at["x"], "z": at["y"]}
    return {"x": at["x"] ^ at["w"], "y": at["y"] + at["z"], "z": at["y"]}


MOVES = pairs_of(AXES, place_target)


def move(block):
    return lax.ppermute(block, AXES, MOVES)


def move_back(block):
    return lax.ppermute(block, AXES, [(b, a) for a, b in MOVES])


def swap_core(block):
    return send(block, ("c",), lambda at: {"c": at["c"] ^ 1})


def swap_x(block):
    return send(block, ("x", "c", "w"), lambda at: {"x": at["x"] ^ 1, "w": at["w"] ^ at["c"]})


def swap_w(block):
    return send(block, ("w",), lambda at: {"w": at["w"] ^ 1})


def ring(block, axis, step):
    return send(block, (axis,), lambda at: {axis: at[axis] + step})


def add(*terms):
    return sum(t.astype(F32) for t in terms)


def mark(array):
    return array[(0,) * array.ndim]


def tie(block, after):
    return block + (after * 0).astype(block.dtype)


def gather(block, after=(None, None, None)):
    n = block.shape[0] // 2
    with jax.named_scope("ring"):
        above, below = ring(block, "y", -1), ring(block, "y", 1)
    with jax.named_scope("own_x"):
        own_x = swap_x(block)
    near = jnp.concatenate([above, below], axis=0)
    near = near if after[0] is None else tie(near, after[0])
    with jax.named_scope("far"):
        far = jnp.concatenate([ring(near[n * 2 : n * 3], "y", 1), ring(near[n : 2 * n], "y", -1)], axis=0)
    far = far if after[1] is None else tie(far, after[1])
    with jax.named_scope("near_x"):
        near_x = swap_x(near)
    with jax.named_scope("far_x"):
        far_x = swap_x(far)
    far_x = far_x if after[2] is None else tie(far_x, after[2])
    return [block, near, far, own_x, near_x, far_x]


def scatter_x(part, after=None):
    later = [] if after is None else [after * 0]
    with jax.named_scope("far_x"):
        far = add(part[3], swap_x(part[7]), *later).astype(BF)
    with jax.named_scope("near_x"):
        near = add(part[1:3], swap_x(part[5:7]), *later)
    with jax.named_scope("own_x"):
        own = add(part[0], swap_x(part[4]), *later)
    return far, near, own


def scatter_far(far, near, after=None):
    m = far.shape[0] // 2
    if after is not None:
        near = tie(near, after)
    with jax.named_scope("far"):
        above = jnp.concatenate([near[0, :m] + ring(far[:m], "y", 1).astype(F32), near[0, m:]], axis=0).astype(BF)
        below = jnp.concatenate([near[1, :m], near[1, m:] + ring(far[m:], "y", -1).astype(F32)], axis=0).astype(BF)
    return above, below


def scatter_near(above, below, own, after=None):
    later = [] if after is None else [after * 0]
    with jax.named_scope("ring"):
        return add(own, ring(above, "y", 1), ring(below, "y", -1), *later)


def mm(a, b, ca=1, cb=0):
    return lax.dot_general(a, b, (((ca,), (cb,)), ((), ())), preferred_element_type=F32)


def turn(head, table, back):
    first = head[:, :LANES]
    n = LANES
    left = pltpu.roll(first, n - 32, 1)
    right = pltpu.roll(first, 32, 1)
    sines = left * table[:, n : 2 * n] + right * table[:, 2 * n :]
    first = first * table[:, :n] + (-sines if back else sines)
    return jnp.concatenate([first, head[:, LANES:]], axis=1)


def whole(shape):
    return pl.BlockSpec(shape, lambda *_: (0,) * len(shape), pipeline_mode=pl.Buffered(1))


def kept(shape):
    return pl.BlockSpec(shape, lambda *_: (0,) * len(shape))


def tiles(*shape, axis=0):
    return pl.BlockSpec(shape, lambda i: tuple(i if a == axis else 0 for a in range(len(shape))))


def anywhere(count):
    return [pl.BlockSpec(memory_space=pl.ANY)] * count


def params():
    return pltpu.CompilerParams(vmem_limit_bytes=VMEM_BYTES, dimension_semantics=("arbitrary",))


def project_kernel(where, x, weights, table, h1, h2, qkv, act, slope, norm, b_sum, cols, small, bias_q, bias_u, sem):
    chip = where[0]
    first = pl.program_id(0) == 0

    @pl.when(first)
    def _():
        pltpu.make_async_copy(weights, cols, sem).start()

    v = x[...].astype(F32)
    center = v - jnp.mean(v, axis=-1, keepdims=True)
    rstd = lax.rsqrt(jnp.mean(center * center, axis=-1, keepdims=True) + NORM_EPS)
    xhat = center * rstd
    q3, half, width = qkv.shape[1], act.shape[2], x.shape[1]
    dim = q3 // 3

    @pl.when(first)
    def _():
        pltpu.make_async_copy(weights, cols, sem).wait()
        for f in range(16):
            small[f] = cols[f % 2, 0, f // 2, :16, q3 + 2 * half :].astype(F32)
            at = slice(f * LANES, (f + 1) * LANES)
            for k, row in enumerate((0, 1, 3, 4)):
                norm[k : k + 1, at] = small[f, row : row + 1]
            b_sum[:, at] = small[f, 2:3] + small[f, 5:6]
        for k in range(6):
            block = (k // 2) * 16 + chip * 2 + k % 2
            bias_q[:, k * LANES : (k + 1) * LANES] = small[lax.div(block, 3), pl.ds(6 + lax.rem(block, 3), 1), :]
        for k in range(8):
            bias_u[:, k * LANES : (k + 1) * LANES] = small[chip * 2 + k // 4, 9 + k % 4 : 10 + k % 4]

    one = (xhat * norm[0:1] + norm[1:2]).astype(BF)
    two = (xhat * norm[2:3] + norm[3:4]).astype(BF)
    h1[...] = one
    h2[...] = two
    step = cols.shape[3]
    mixed = jnp.broadcast_to(bias_q[...], (v.shape[0], q3))
    for h in range(8):
        mixed += mm(one[:, h * 256 : (h + 1) * 256], cols[:, :, h, :, :q3].reshape(8 * step, -1))
    qkv[:, :dim] = turn(mixed[:, :dim], table[...], False).astype(BF)
    qkv[:, dim : 2 * dim] = turn(mixed[:, dim : 2 * dim], table[...], False).astype(BF)
    qkv[:, 2 * dim :] = mixed[:, 2 * dim :].astype(BF)
    for part in range(2):
        pre = jnp.broadcast_to(bias_u[:, part * half : (part + 1) * half], (v.shape[0], half))
        start = q3 + part * half
        for h in range(8):
            pre += mm(two[:, h * 256 : (h + 1) * 256], cols[:, :, h, :, start : start + half].reshape(8 * step, -1))
        phi = 0.5 * (1.0 + lax.erf(pre * 0.7071067811865476))
        act[part] = (pre * phi).astype(BF)
        slope[part] = (phi + pre * jnp.exp(-0.5 * pre * pre) * 0.3989422804014327).astype(BF)


def project(where, x, weights, table, q3, ff):
    n, width = x.shape

    def rows(*shape, axis=0):
        return pl.BlockSpec(shape, lambda i, s: tuple(i if a == axis else 0 for a in range(len(shape))))

    return pl.pallas_call(
        project_kernel,
        grid_spec=pltpu.PrefetchScalarGridSpec(
            num_scalar_prefetch=1,
            grid=(n // TILE,),
            in_specs=[rows(TILE, width), *anywhere(1), rows(TILE, 3 * LANES)],
            out_specs=[
                rows(TILE, width), rows(TILE, width), rows(TILE, q3), rows(2, TILE, ff // 2, axis=1),
                rows(2, TILE, ff // 2, axis=1), kept((4, width)), kept((1, width)),
            ],
            scratch_shapes=[
                pltpu.VMEM(weights.shape, BF), pltpu.VMEM((16, 16, LANES), F32), pltpu.VMEM((1, q3), F32),
                pltpu.VMEM((1, ff), F32), pltpu.SemaphoreType.DMA,
            ],
        ),
        out_shape=[
            jax.ShapeDtypeStruct((n, width), BF), jax.ShapeDtypeStruct((n, width), BF), jax.ShapeDtypeStruct((n, q3), BF),
            jax.ShapeDtypeStruct((2, n, ff // 2), BF), jax.ShapeDtypeStruct((2, n, ff // 2), BF),
            jax.ShapeDtypeStruct((4, width), F32), jax.ShapeDtypeStruct((1, width), F32),
        ],
        compiler_params=params(),
        cost_estimate=pl.CostEstimate(flops=2 * n * width * (q3 + ff), bytes_accessed=30 << 20, transcendentals=2 * n * ff),
        name="project",
    )(where, x, weights, table)


def attend_kernel(q, kv, place_q, place_k, doc_q, doc_k, prob, att):
    dim = kv.shape[1] // 3
    key, value = kv[:, dim : 2 * dim], kv[:, 2 * dim :]
    scores = mm(q[:, :dim], key, 1, 1) * (dim ** -0.5)
    pq, pk = place_q[...], place_k[...]
    allowed = ((doc_q[...] == doc_k[...]) & (pk <= pq)) | (pk == pq)
    scores = jnp.where(allowed, scores, MASKED)
    expo = jnp.exp(scores - jnp.max(scores, axis=-1, keepdims=True))
    p = (expo * (1.0 / jnp.sum(expo, axis=-1, keepdims=True))).astype(BF)
    prob[...] = p
    out = mm(p, value).astype(BF)
    att[0] = out[:, : dim // 2]
    att[1] = out[:, dim // 2 :]


def attend(qkv, places, docs):
    n, q3 = qkv.shape
    dim = q3 // 3
    doc_k = jnp.where(docs < 0, -2, docs)
    return pl.pallas_call(
        attend_kernel,
        grid=(n // TILE,),
        in_specs=[tiles(TILE, q3), whole((n, q3)), tiles(TILE, 1), whole((1, n)), tiles(TILE, 1), whole((1, n))],
        out_specs=[tiles(TILE, n), tiles(2, TILE, dim // 2, axis=1)],
        out_shape=[jax.ShapeDtypeStruct((n, n), BF), jax.ShapeDtypeStruct((2, n, dim // 2), BF)],
        compiler_params=params(),
        cost_estimate=pl.CostEstimate(flops=4 * n * n * dim, bytes_accessed=5 << 20, transcendentals=n * n),
        name="attend",
    )(qkv, qkv, places[:, None], places[None], docs[:, None], doc_k[None])


def attend_back_kernel(q, kv, prob, g, table_q, table, *rest):
    out, key_sum, value_sum = rest[-3:]
    i = pl.program_id(0)
    n = kv.shape[0]
    dim = kv.shape[1] // 3
    key, value = kv[:, dim : 2 * dim], kv[:, 2 * dim :]
    g_tile = jnp.concatenate([g[0], g[1]], axis=1)
    p_low = prob[...]
    p = p_low.astype(F32)
    g_prob = mm(g_tile, value, 1, 1)
    inner = jnp.sum(p * g_prob, axis=-1, keepdims=True)
    g_scores = (p * (g_prob - inner)).astype(BF)
    scale = dim ** -0.5
    g_query = mm(g_scores, key) * scale
    out[pl.ds(i * TILE, TILE), :dim] = turn(g_query, table_q[...], True).astype(BF)
    g_key = mm(g_scores, q[:, :dim], 0, 0)
    g_value = mm(p_low, g_tile, 0, 0)

    @pl.when(i == 0)
    def _():
        key_sum[...] = g_key
        value_sum[...] = g_value

    @pl.when(i > 0)
    def _():
        key_sum[...] += g_key
        value_sum[...] += g_value

    @pl.when(i == pl.num_programs(0) - 1)
    def _():
        out[:, dim : 2 * dim] = turn(key_sum[...] * scale, table[...], True).astype(BF)
        out[:, 2 * dim :] = value_sum[...].astype(BF)


def attend_back(qkv, prob, g_att, table, after):
    n, q3 = qkv.shape
    dim = q3 // 3
    return pl.pallas_call(
        attend_back_kernel,
        grid=(n // TILE,),
        in_specs=[
            tiles(TILE, q3), whole((n, q3)), tiles(TILE, n), tiles(2, TILE, dim // 2, axis=1), tiles(TILE, 3 * LANES),
            whole((n, 3 * LANES)), *anywhere(len(after)),
        ],
        out_specs=kept((n, q3)),
        out_shape=jax.ShapeDtypeStruct((n, q3), BF),
        scratch_shapes=[pltpu.VMEM((n, dim), F32), pltpu.VMEM((n, dim), F32)],
        compiler_params=params(),
        cost_estimate=pl.CostEstimate(flops=8 * n * n * dim, bytes_accessed=8 << 20, transcendentals=0),
        name="attend_back",
    )(qkv, qkv, prob, g_att, table, table, *after)


def branch_grad_kernel(core, g, mine, twin, slope, *rest):
    g_pre, g_att, bias = rest[-3:]
    c = core[0]
    half = slope.shape[2]
    own = mm(g[...], mine[...], 1, 1)
    other = mm(g[...], twin[...], 1, 1)

    @pl.when(pl.program_id(0) == 0)
    def _():
        bias[...] = jnp.zeros_like(bias)

    for at, part in ((c, own), (1 - c, other)):
        pre = (part[:, :half] * slope[at].astype(F32)).astype(BF)
        g_pre[at] = pre
        g_att[at] = part[:, half:].astype(BF)
        bias[at] += jnp.sum(pre.astype(F32), axis=0, keepdims=True)


def branch_grad(core, g, mine, twin, slope, after):
    n, width = g.shape
    half = slope.shape[2]
    tail = mine.shape[0] - half
    return pl.pallas_call(
        branch_grad_kernel,
        grid_spec=pltpu.PrefetchScalarGridSpec(
            num_scalar_prefetch=1,
            grid=(n // TILE,),
            in_specs=[
                pl.BlockSpec((TILE, width), lambda i, s: (i, 0)), whole(mine.shape), whole(twin.shape),
                pl.BlockSpec((2, TILE, half), lambda i, s: (0, i, 0)), *anywhere(len(after)),
            ],
            out_specs=[
                pl.BlockSpec((2, TILE, half), lambda i, s: (0, i, 0)),
                pl.BlockSpec((2, TILE, tail), lambda i, s: (0, i, 0)), kept((2, 1, half)),
            ],
        ),
        out_shape=[
            jax.ShapeDtypeStruct((2, n, half), BF), jax.ShapeDtypeStruct((2, n, tail), BF),
            jax.ShapeDtypeStruct((2, 1, half), F32),
        ],
        compiler_params=params(),
        cost_estimate=pl.CostEstimate(flops=4 * n * width * (half + tail), bytes_accessed=16 << 20, transcendentals=0),
        name="branch_grad",
    )(core, g, mine, twin, slope, *after)


def branches_kernel(core, act, att, mine, twin, out):
    c = core[0]
    half = act.shape[2]
    own, other = (jnp.concatenate([act[k], att[k]], axis=1) for k in (c, 1 - c))
    total = mm(own, mine[...]) + mm(other, twin[...])
    out[...] = total.astype(BF).reshape(out.shape)


def branches_out(core, act, att, mine, twin):
    half, tail = act.shape[2], att.shape[2]
    n, width = act.shape[1], mine.shape[1]
    return pl.pallas_call(
        branches_kernel,
        grid_spec=pltpu.PrefetchScalarGridSpec(
            num_scalar_prefetch=1,
            grid=(n // TILE,),
            in_specs=[
                pl.BlockSpec((2, TILE, half), lambda i, s: (0, i, 0)), pl.BlockSpec((2, TILE, tail), lambda i, s: (0, i, 0)),
                whole(mine.shape), whole(twin.shape),
            ],
            out_specs=pl.BlockSpec((TILE // 128, 128, width), lambda i, s: (i, 0, 0)),
        ),
        out_shape=jax.ShapeDtypeStruct((n // 128, 128, width), BF),
        compiler_params=params(),
        cost_estimate=pl.CostEstimate(flops=4 * n * width * (half + tail), bytes_accessed=14 << 20, transcendentals=0),
        name="branches",
    )(core, act, att, mine, twin)


def partials_kernel(where, x, norm, g_mixed, g_pre, u_bias, dy_sum, weights, *rest):
    part, cols, sums, bias, sem = rest[-5:]
    chip = where[0]
    first = pl.program_id(0) == 0

    @pl.when(first)
    def _():
        pltpu.make_async_copy(weights, cols, sem).start()
        sums[...] = jnp.zeros_like(sums)
        bias[...] = jnp.zeros_like(bias)

    v = x[...].astype(F32)
    center = v - jnp.mean(v, axis=-1, keepdims=True)
    rstd = lax.rsqrt(jnp.mean(center * center, axis=-1, keepdims=True) + NORM_EPS)
    xhat = center * rstd
    step = cols.shape[3]
    half, q3 = g_pre.shape[2], g_mixed.shape[1]
    gm = g_mixed[...]
    gm_sum = jnp.sum(gm.astype(F32), axis=0, keepdims=True)
    for k in range(6):
        bias[k : k + 1] += gm_sum[:, k * LANES : (k + 1) * LANES]

    @pl.when(first)
    def _():
        pltpu.make_async_copy(weights, cols, sem).wait()

    n = 128
    slots = v.shape[0] // n
    i = pl.program_id(0)
    for h in range(8):
        at = slice(h * 256, (h + 1) * 256)
        wide = cols[:, :, h].reshape(8 * step, -1)
        one = mm(gm, wide[:, :q3], 1, 1)
        two = mm(g_pre[0], wide[:, q3 : q3 + half], 1, 1) + mm(g_pre[1], wide[:, q3 + half : q3 + 2 * half], 1, 1)
        e = (one * norm[0:1, at] + two * norm[2:3, at]).astype(BF)
        for s in range(slots):
            part[i * slots + s, :n, at] = e[s * n : (s + 1) * n]
        xh = xhat[:, at]
        sums[h, 0:1] += jnp.sum(one * xh, axis=0, keepdims=True)
        sums[h, 1:2] += jnp.sum(one, axis=0, keepdims=True)
        sums[h, 2:3] += jnp.sum(two * xh, axis=0, keepdims=True)
        sums[h, 3:4] += jnp.sum(two, axis=0, keepdims=True)

    @pl.when(i == pl.num_programs(0) - 1)
    def _():
        more = part.shape[1] - n
        for slot in range(8):
            to = where[2 + slot]
            row = [sums[to, k : k + 1] for k in range(4)] + [dy_sum[to]]
            for j in range(6):
                block = to * 6 + j
                section, rest_of = lax.div(block, 16), lax.rem(block, 16)
                value = bias[pl.ds(section * 2 + lax.rem(rest_of, 2), 1), :]
                row.append(jnp.where(lax.div(rest_of, 2) == chip, value, 0.0))
            row = jnp.concatenate(row, axis=1)
            if slot == 0:
                other = jnp.concatenate([u_bias[0], u_bias[1], jnp.zeros((1, row.shape[1] - 2 * half), F32)], axis=1)
            else:
                other = jnp.zeros_like(row)
            block = jnp.concatenate([row, other, jnp.zeros((more - 2, row.shape[1]), F32)], axis=0)
            part[slot, n:, :] = block.astype(BF)


def partials(where, x, norm, g_mixed, g_pre, u_bias, dy_sum, weights, after):
    n, width = x.shape
    half, q3 = g_pre.shape[2], g_mixed.shape[1]

    def rows(*shape, axis=0):
        return pl.BlockSpec(shape, lambda i, s: tuple(i if a == axis else 0 for a in range(len(shape))))

    return pl.pallas_call(
        partials_kernel,
        grid_spec=pltpu.PrefetchScalarGridSpec(
            num_scalar_prefetch=1,
            grid=(n // TILE,),
            in_specs=[
                rows(TILE, width), whole(norm.shape), rows(TILE, q3), rows(2, TILE, half, axis=1), whole(u_bias.shape),
                whole(dy_sum.shape), *anywhere(1 + len(after)),
            ],
            out_specs=kept((n // 128, 144, width)),
            scratch_shapes=[
                pltpu.VMEM(weights.shape, BF), pltpu.VMEM((8, 8, 256), F32), pltpu.VMEM((8, LANES), F32),
                pltpu.SemaphoreType.DMA,
            ],
        ),
        out_shape=jax.ShapeDtypeStruct((n // 128, 144, width), BF),
        compiler_params=params(),
        cost_estimate=pl.CostEstimate(flops=2 * n * width * (q3 + 2 * half), bytes_accessed=24 << 20, transcendentals=0),
        name="partials",
    )(where, x, norm, g_mixed, g_pre, u_bias, dy_sum, weights, *after)


def half_grad_kernel(core, left, right, *rest):
    keep, give, pair = rest[-3:]
    c = core[0]
    n = pair.shape[1]
    step = n // 4
    done = 0
    for part in range(right.shape[0]):
        res = mm(left[...], right[part], 0, 0).astype(BF)
        w = res.shape[1]
        pair[0, :, done : done + w] = res[:n]
        pair[1, :, done : done + w] = res[n:]
        done += w
    for z in range(4):
        at = slice(z * step, (z + 1) * step)
        keep[z, 0] = pair[c, at]
        give[z, 0] = pair[1 - c, at]


def half_grad(core, left, right, after):
    n, width = left.shape
    cols = right.shape[2] * right.shape[0]
    rows = width // 16
    return pl.pallas_call(
        half_grad_kernel,
        grid_spec=pltpu.PrefetchScalarGridSpec(
            num_scalar_prefetch=1,
            grid=(8,),
            in_specs=[pl.BlockSpec((n, 2 * rows), lambda i, s: (0, i)), whole(right.shape), *anywhere(len(after))],
            out_specs=[pl.BlockSpec((4, 1, rows // 4, cols), lambda i, s: (0, i, 0, 0))] * 2,
            scratch_shapes=[pltpu.VMEM((2, rows, cols), BF)],
        ),
        out_shape=[jax.ShapeDtypeStruct((4, 8, rows // 4, cols), BF)] * 2,
        compiler_params=params(),
        cost_estimate=pl.CostEstimate(flops=2 * n * width * cols, bytes_accessed=12 << 20, transcendentals=0),
        name="half_grad",
    )(core, left, right, *after)


def rows_grad_kernel(core, act, att, g, *rest):
    keep, give = rest[-2:]
    whole_g = g[...]
    act_t = mm(act[0], whole_g, 0, 0).astype(BF)
    att_t = mm(att[0], whole_g, 0, 0).astype(BF)
    a, b = act_t.shape[0] // 8, att_t.shape[0] // 8
    for p, out in enumerate((give, keep)):
        @pl.when(pl.program_id(0) == p)
        def _():
            for i in range(8):
                out[i // 4, i % 4, :a] = act_t[i * a : (i + 1) * a]
                out[i // 4, i % 4, a:] = att_t[i * b : (i + 1) * b]


def rows_grad(core, act, att, g, after):
    n, width = g.shape
    half, tail = act.shape[2], att.shape[2]
    shape = (2, 4, (half + tail) // 8, width)
    return pl.pallas_call(
        rows_grad_kernel,
        grid_spec=pltpu.PrefetchScalarGridSpec(
            num_scalar_prefetch=1,
            grid=(2,),
            in_specs=[
                pl.BlockSpec((1, n, half), lambda p, s: (s[0] * p + (1 - s[0]) * (1 - p), 0, 0)),
                pl.BlockSpec((1, n, tail), lambda p, s: (s[0] * p + (1 - s[0]) * (1 - p), 0, 0)), whole(g.shape),
                *anywhere(len(after)),
            ],
            out_specs=[kept(shape), kept(shape)],
        ),
        out_shape=[jax.ShapeDtypeStruct(shape, BF)] * 2,
        compiler_params=params(),
        cost_estimate=pl.CostEstimate(flops=4 * n * width * (half + tail), bytes_accessed=14 << 20, transcendentals=0),
        name="rows_grad",
    )(core, act, att, g, *after)


def columns_out_kernel(where, *refs):
    blocks, (qkv, up) = refs[:4], refs[4:]
    a, w = pl.program_id(0), pl.program_id(1)
    offset = lax.rem(where[0] - a + 4, 4)
    at = jnp.where(w == where[1], 0, 1)
    dim, part = qkv.shape[1] // 24, up.shape[1] // 8
    for k, b in enumerate(blocks):
        @pl.when(offset == k)
        def _():
            for h in range(8):
                for s in range(3):
                    to = (s * 8 + h) * dim
                    qkv[:, to : to + dim] = b[at, h, :, s * dim : (s + 1) * dim].astype(F32)
                up[:, h * part : (h + 1) * part] = b[at, h, :, 3 * dim :].astype(F32)


def columns_out(where, blocks, q3, ff):
    rows = blocks[0].shape[2]
    return pl.pallas_call(
        columns_out_kernel,
        grid_spec=pltpu.PrefetchScalarGridSpec(
            num_scalar_prefetch=1,
            grid=(4, 2),
            in_specs=[whole(b.shape) for b in blocks],
            out_specs=[pl.BlockSpec((rows, n), lambda a, w, s: (a * 2 + w, 0)) for n in (8 * q3, 8 * ff)],
        ),
        out_shape=[jax.ShapeDtypeStruct((8 * rows, n), F32) for n in (8 * q3, 8 * ff)],
        compiler_params=pltpu.CompilerParams(vmem_limit_bytes=VMEM_BYTES),
        cost_estimate=pl.CostEstimate(flops=0, bytes_accessed=12 << 20, transcendentals=0),
        name="columns_out",
    )(where, *blocks)


def rows_out_kernel(where, mine, twin, down, out):
    w, a = pl.program_id(0), pl.program_id(1)
    offset = lax.rem(where[0] - a + 4, 4)
    n = down.shape[0]
    for k, b in enumerate((mine, twin)):
        @pl.when((w == where[1]) == (k == 0))
        def _():
            v = b[offset]
            down[...] = v[:n].astype(F32)
            out[...] = v[n:].astype(F32)


def rows_out(where, mine, twin):
    _, n, width = mine.shape
    cut = n * 4 // 5
    return pl.pallas_call(
        rows_out_kernel,
        grid_spec=pltpu.PrefetchScalarGridSpec(
            num_scalar_prefetch=1,
            grid=(2, 4),
            in_specs=[whole(mine.shape), whole(twin.shape)],
            out_specs=[
                pl.BlockSpec((cut, width), lambda w, a, s: (w * 4 + a, 0)),
                pl.BlockSpec((n - cut, width), lambda w, a, s: (w * 4 + a, 0)),
            ],
        ),
        out_shape=[jax.ShapeDtypeStruct((8 * cut, width), F32), jax.ShapeDtypeStruct((8 * (n - cut), width), F32)],
        compiler_params=pltpu.CompilerParams(vmem_limit_bytes=VMEM_BYTES),
        cost_estimate=pl.CostEstimate(flops=0, bytes_accessed=8 << 20, transcendentals=0),
        name="rows_out",
    )(where, mine, twin)


def small_out_kernel(where, total, norms, q_bias, u_bias):
    core = where[1]
    for k in range(5):
        pair = [total[0:1, (2 * k + c) * LANES : (2 * k + c + 1) * LANES] for c in range(2)]
        norms[k : k + 1] = jnp.where(core == 0, pair[0], pair[1])
    for j in range(3):
        pair = [total[0:1, (10 + 3 * c + j) * LANES : (11 + 3 * c + j) * LANES] for c in range(2)]
        q_bias[j : j + 1] = jnp.where(core == 0, pair[0], pair[1])
    for j in range(4):
        pair = [total[1:2, (4 * c + j) * LANES : (4 * c + j + 1) * LANES] for c in range(2)]
        u_bias[j : j + 1] = jnp.where(core == 0, pair[0], pair[1])


def small_out(where, total):
    return pl.pallas_call(
        small_out_kernel,
        in_specs=[pl.BlockSpec(memory_space=pltpu.SMEM), pl.BlockSpec(memory_space=pltpu.VMEM)],
        out_specs=[pl.BlockSpec(memory_space=pltpu.VMEM)] * 3,
        out_shape=[jax.ShapeDtypeStruct((n, LANES), F32) for n in (5, 3, 4)],
        name="small_out",
    )(where, total)


def pair_sum(keep, give, swap, after=None):
    later = [] if after is None else [after * 0]
    return add(keep, swap(give), *later).astype(BF)


def copies_scatter(pieces, after=None):
    z = lax.axis_index("z")
    later = [] if after is None else [after * 0]

    def piece(offset):
        return lax.dynamic_index_in_dim(pieces, (z + offset) % 4, 0, keepdims=False)

    return add(piece(0), *(ring(piece(o), "z", o) for o in (1, 2, 3)), *later)


def copies_gather(piece):
    return [piece] + [ring(piece, "z", o) for o in (1, 2, 3)]


def body(
    tokens, segment_ids, out_cotangent, ln1_gain, ln1_bias, qkv_weight, qkv_bias, out_weight, out_bias,
    ln2_gain, ln2_bias, up_weight, up_bias, down_weight, down_bias,
):
    _, shard, width = tokens.shape
    head_dim = width // HEADS
    ff = up_weight.shape[1]
    ff_part = ff // 8
    rows = qkv_weight.shape[0]
    x, y, core, w, z = (lax.axis_index(a) for a in AXES)
    chip = x * 4 + y
    core_at = core.astype(jnp.int32).reshape(1)
    copy_at = jnp.stack([z, w]).astype(jnp.int32)
    chip_at = jnp.stack([chip, core]).astype(jnp.int32)

    with jax.named_scope("x"):
        x_own = move(tokens[0])
        x_parts = gather(x_own)
    with jax.named_scope("ids"):
        ids = move(segment_ids)[0]
    x_all = jnp.concatenate(x_parts, axis=0)
    with jax.named_scope("dy"):
        g_own = move(tie(out_cotangent[0], x_own[0, 0]))

    step = rows // 4
    q_part, u_part = (lax.dynamic_slice_in_dim(m, z * step, step, 0) for m in (qkv_weight, up_weight))
    q_part = q_part.reshape(step, 3, 8, head_dim).transpose(2, 0, 1, 3).reshape(8, step, 3 * head_dim)
    u_part = u_part.reshape(step, 8, ff_part).transpose(1, 0, 2)
    small = jnp.concatenate([ln1_gain, ln1_bias, out_bias, ln2_gain, ln2_bias, down_bias, qkv_bias, up_bias])
    n_small = small.shape[0] // LANES
    small = jnp.pad(small.reshape(n_small, LANES), ((0, step - n_small), (0, 0)))
    cols = jnp.concatenate([q_part, u_part, jnp.broadcast_to(small[None], (8, step, LANES))], axis=2)
    with jax.named_scope("weights"):
        cols = lax.all_to_all(cols, CHIPS, 0, 0, tiled=True)
        cols = lax.all_gather(tie(cols, mark(x_own)), ("c", "z"), axis=0).reshape(2, 4, *cols.shape)
    w_mine = jnp.concatenate([down_weight, out_weight], axis=0)
    with jax.named_scope("row_weights"):
        w_twin = swap_core(w_mine)

    y_offset = jnp.array([0, 1, 3, 2], jnp.int32)
    slot = jnp.arange(8, dtype=jnp.int32)
    slot_chip = (x ^ (slot // 4)) * 4 + (y + y_offset[slot % 4]) % 4
    slot_at = jnp.concatenate([chip_at, slot_chip.astype(jnp.int32)])
    group = w ^ (x & core)
    block = ((x ^ (group & core)) ^ (slot // 4)) * 4 + (y - z + y_offset[slot % 4] + 4) % 4
    places = (block[:, None] * shard + jnp.arange(shard, dtype=jnp.int32)[None, :]).reshape(8 * shard)
    half = ROTARY // 2
    lane = jnp.arange(LANES, dtype=jnp.int32)[None]
    freqs = jnp.exp((lane % half).astype(F32) * (-2.0 * math.log(10000.0) / ROTARY))
    angles = places.astype(F32)[:, None] * freqs
    sin = jnp.sin(angles)
    table = jnp.concatenate(
        [
            jnp.where(lane < ROTARY, jnp.cos(angles), 1.0), jnp.where(lane < half, -sin, 0.0),
            jnp.where((lane >= half) & (lane < ROTARY), sin, 0.0),
        ],
        axis=1,
    )
    docs = jnp.take(ids.reshape(8, shard), block, axis=0).reshape(8 * shard)

    h1, h2, qkv, act, slope, norm, b_sum = project(chip_at, x_all, cols, table, 3 * head_dim, ff_part)
    prob, attended = attend(qkv, places, docs)
    out_part = branches_out(core_at, act, attended, w_mine, w_twin)
    with jax.named_scope("dy"):
        g_parts = gather(tie(g_own, mark(x_parts[2])), (mark(qkv), mark(attended), mark(out_part)))
    g_all = jnp.concatenate(g_parts, axis=0)

    g_pre, g_att, up_bias_grad = branch_grad(core_at, g_all, w_mine, w_twin, slope, (out_part,))
    with jax.named_scope("out"):
        out_far, out_near, out_own = scatter_x(out_part, mark(up_bias_grad))
    rows_keep, rows_give = rows_grad(core_at, act, attended, g_all, (g_pre, out_far))
    with jax.named_scope("out"):
        out_above, out_below = scatter_far(out_far, out_near, mark(rows_give).astype(F32))
    g_mixed = attend_back(qkv, prob, g_att, table, (rows_give, out_above, out_below))
    with jax.named_scope("out"):
        out_sum = scatter_near(out_above, out_below, out_own, mark(g_mixed).astype(F32))
    with jax.named_scope("rows/core"):
        rows_part = pair_sum(rows_keep, rows_give, swap_core, mark(g_mixed).astype(F32))
    x_rows = x_own.astype(F32)
    layer_output = (x_rows + out_sum + b_sum).astype(BF)
    qkv_keep, qkv_give = half_grad(core_at, h1, g_mixed[None], (layer_output, rows_part))
    with jax.named_scope("out/back"):
        layer_output = move_back(layer_output)
    up_keep, up_give = half_grad(core_at, h2, g_pre, (qkv_give,))
    with jax.named_scope("rows/w"):
        rows_part = pair_sum(
            lax.dynamic_index_in_dim(rows_part, w, 0, keepdims=False),
            lax.dynamic_index_in_dim(rows_part, 1 - w, 0, keepdims=False), swap_w, mark(up_give).astype(F32),
        )
    with jax.named_scope("qkv/core"):
        qkv_part = pair_sum(qkv_keep, qkv_give, swap_core, mark(up_give).astype(F32))
    dy_sum = jnp.sum(g_own.astype(F32), axis=0).reshape(8, 1, 256)
    part = partials(slot_at, x_all, norm, g_mixed, g_pre, up_bias_grad, dy_sum, cols, (up_give, qkv_part, rows_part))
    last = mark(part).astype(F32)

    with jax.named_scope("up/core"):
        up_part = pair_sum(up_keep, up_give, swap_core, last)
    with jax.named_scope("rows/z"):
        rows_part = copies_scatter(rows_part, last).astype(BF)
    with jax.named_scope("qkv/z"):
        qkv_part = copies_scatter(qkv_part, last).astype(BF)
    with jax.named_scope("up/z"):
        up_part = copies_scatter(up_part).astype(BF)
    with jax.named_scope("rows/z_back"):
        rows_part = jnp.stack(copies_gather(rows_part))
    with jax.named_scope("rows/w_back"):
        rows_twin = swap_w(rows_part)
    grad_down, grad_out = rows_out(copy_at, rows_part, rows_twin)
    columns = jnp.concatenate([qkv_part, up_part], axis=2).reshape(8, 2, step // 2, -1)
    with jax.named_scope("columns/w"):
        piece = pair_sum(
            lax.dynamic_index_in_dim(columns, w, 1, keepdims=False),
            lax.dynamic_index_in_dim(columns, 1 - w, 1, keepdims=False), swap_w,
        )
    with jax.named_scope("columns/chips"):
        piece = lax.all_to_all(piece, CHIPS, 0, 0, tiled=True)
    with jax.named_scope("columns/w_back"):
        both = jnp.stack([piece, swap_w(piece)])
    with jax.named_scope("columns/z_back"):
        blocks = copies_gather(both)
    grad_qkv, grad_up = columns_out(copy_at, blocks, 3 * head_dim, ff_part)

    with jax.named_scope("part"):
        far, near, own = scatter_x(part)
        total = scatter_near(*scatter_far(far, near), own)
    center = x_rows - jnp.mean(x_rows, axis=-1, keepdims=True)
    rstd = lax.rsqrt(jnp.mean(center * center, axis=-1, keepdims=True) + NORM_EPS)
    xhat = center * rstd
    e = total[:shard]
    grad_x = rstd * (e - jnp.mean(e, axis=-1, keepdims=True) - xhat * jnp.mean(e * xhat, axis=-1, keepdims=True))
    input_grad = (g_own.astype(F32) + grad_x).astype(BF)
    with jax.named_scope("part/back"):
        input_grad = move_back(input_grad)

    sums = total[shard : shard + 2]
    with jax.named_scope("small/z"):
        sums = add(sums, ring(sums, "z", 1), ring(sums, "z", 2), ring(sums, "z", 3))
    with jax.named_scope("small/w"):
        sums = add(sums, swap_w(sums))
    with jax.named_scope("small/core"):
        sums = add(sums, swap_core(sums))
    norms, grad_qb, grad_ub = small_out(chip_at, sums)

    return (
        layer_output[None], input_grad[None], norms[0], norms[1], grad_qkv, grad_qb.reshape(-1), grad_out,
        norms[4], norms[2], norms[3], grad_up, grad_ub.reshape(-1), grad_down, norms[4],
    )


def solution(mesh):
    fine = Mesh(mesh.devices.reshape(*SIZES.values()), AXES)
    by_owner, by_place = ("x", "y", "c"), ("w", "z")
    act, vec, mat = P(by_owner, by_place, None), P(by_owner), P(by_owner, None)
    return jax.shard_map(
        body,
        mesh=fine,
        in_specs=(act, mat, act, vec, vec, mat, vec, mat, vec, vec, vec, mat, vec, mat, vec),
        out_specs=(act, act, vec, vec, mat, vec, mat, vec, vec, vec, mat, vec, mat, vec),
        check_vma=False,
    )
```

time: 910 us -> 504 us (0.55)
  waiting for transfers between devices: 611 us -> 140 us
  Pallas kernels: 0 us -> 123 us
  matrix products: 85.5 us -> 0 us
  starting transfers between devices: 59.6 us -> 117 us
  blocking collectives: 30.3 us -> 0 us
  other arithmetic: 54.5 us -> 43.2 us
    psum x2 -> x0, waiting for transfers between devices: 264 us -> none  [the longest x1 138 us: body(): sums = lax.psum(sums, ('x', 'y', 'c', 'w', 'z'))]
    reduce_scatter x4 -> x0, waiting for transfers between devices: 180 us -> none  [the longest x2 79.1 us: by_columns(): own = lax.psum_scatter(own, COPIES, scatter_dimension=0, tiled=True)]
    pallas_call x0 -> x12, Pallas kernels: none -> 123 us  [the longest x2 19.8 us: half_grad(): pl.pallas_call(half_grad_kernel, grid_spec=pltpu.PrefetchScalarGridSpec(n...]
    all_gather x4 -> x1, waiting for transfers between devices: 94.2 us -> 0.01 us  [body(): lax.all_gather(tie(cols, mark(x_own)), ('c', 'z'), axis=0)]
    dot_general x15 -> x0, matrix products: 85.5 us -> none  [dot(): return lax.dot_general(a, b, (dims, ((), ())), preferred_element_type=F32)]
    ppermute x13 -> x61, starting transfers between devices: 19.5 us -> 104 us  [the longest x56 75.9 us: send(): return lax.ppermute(block, axes, pairs_of(axes, target))]
    ppermute x13 -> x61, waiting for transfers between devices: 72.6 us -> 140 us  [the longest x56 97.3 us: send(): return lax.ppermute(block, axes, pairs_of(axes, target))]
    all_to_all x3 -> x2, starting transfers between devices: 39.5 us -> 12.6 us  [the longest x1 6.58 us: body(): piece = lax.all_to_all(piece, CHIPS, 0, 0, tiled=True)]
  transfers between devices with their start and end apart: 26 -> 64, of which waited for: 12 -> 20; matrix products, arithmetic and copies ran while one was open for 16% -> 16% of each run, Pallas kernels for 0% -> 23%
where the time goes in v2:
time: 504 us; the launch traced here: 494 us
  waiting for transfers between devices  140 us (28%)
  Pallas kernels  123 us (24%)
  starting transfers between devices  117 us (23%)
  local copies, waits for them, and re-layouts  48.8 us (10%)
  other arithmetic  43.2 us (9%)
  between operations  22 us (4%)
    ppermute x56, waiting for transfers between devices, send(): return lax.ppermute(block, axes, pairs_of(axes, target))  97.3 us
    ppermute x56, starting transfers between devices, send(): return lax.ppermute(block, axes, pairs_of(axes, target))  75.9 us
    ppermute x2, waiting for transfers between devices, move_back(): return lax.ppermute(block, AXES, [(b, a) for a, b in MOVES])  22.7 us
    unnamed x88, local copies, waits for them, and re-layouts  20.5 us
    ppermute x3, waiting for transfers between devices, move(): return lax.ppermute(block, AXES, MOVES)  19.9 us
    pallas_call x2, Pallas kernels, half_grad(): pl.pallas_call(half_grad_kernel, grid_spec=pltpu.PrefetchScalarGridSpec(n...  19.8 us
    pallas_call x1, Pallas kernels, partials(): pl.pallas_call(partials_kernel, grid_spec=pltpu.PrefetchScalarGridSpec(nu...  19.1 us
    ppermute x2, starting transfers between devices, move_back(): return lax.ppermute(block, AXES, [(b, a) for a, b in MOVES])  18.8 us
  transfers between devices with their start and end apart: 64, of which 20 were waited for; matrix products, arithmetic and copies ran while one was open for 16% of the time, Pallas kernels for 23%

profile of v2, /device:TPU:8, one launch (start us, length us, event | category | flops | bytes accessed | tf_op | source)
XLA Modules:
  0.0 494.1 jit_solution(14976283879687688977)
XLA Ops:
  13.2 6.0 %all-to-all-start = ((bf16[8,32,1920]{2,1,0:T(8,128)(2,1)}), bf16[8,32,1920]{2,1,0:T(8,128)(2,1)S(1)}, u32[]{:S(2)}, u32[]{:S(2)}) async-start(bf16[8,32,1920]{2,1,0:T(8,128)(2,1)} %copy.44), calls=%async_computation | async-start | bytes 1966080 | tf_op jit(solution)/shard_map/weights/all_to_all | solution.py:718
  23.0 19.9 %collective-permute-done = bf16[128,2048]{1,0:T(8,128)(2,1)S(1)} collective-permute-done((bf16[128,2048]{1,0:T(8,128)(2,1)S(1)}, bf16[128,2048]{1,0:T(8,128)(2,1)S(1)}, u32[]{:S(2)}, u32[]{:S(2)}) %collective-permute-start) | collective-permute-done | bytes 524320 | tf_op jit(solution)/shard_map/x/ppermute | solution.py:53
  63.3 5.3 %collective-permute-start.2 = (bf16[128,2048]{1,0:T(8,128)(2,1)S(1)}, bf16[128,2048]{1,0:T(8,128)(2,1)S(1)}, u32[]{:S(2)}, u32[]{:S(2)}) collective-permute-start(bf16[128,2048]{1,0:T(8,128)(2,1)S(1)} %collective-permute-done), channel_id=1, source_target_pairs={{0,16},{16,32},{32,48},{48,0},{1,17},{17,33},{33,49},{49,1},{2,18}... | collective-permute-start | bytes 1572872 | tf_op jit(solution)/shard_map/x/ring/ppermute | solution.py:40
  69.7 11.2 %collective-permute-done.2 = bf16[128,2048]{1,0:T(8,128)(2,1)S(1)} collective-permute-done((bf16[128,2048]{1,0:T(8,128)(2,1)S(1)}, bf16[128,2048]{1,0:T(8,128)(2,1)S(1)}, u32[]{:S(2)}, u32[]{:S(2)}) %collective-permute-start.2) | collective-permute-done | bytes 524320 | tf_op jit(solution)/shard_map/x/ring/ppermute | solution.py:40
  99.2 5.2 %collective-permute-done.6 = bf16[256,2048]{1,0:T(8,128)(2,1)S(1)} collective-permute-done((bf16[256,2048]{1,0:T(8,128)(2,1)S(1)}, bf16[256,2048]{1,0:T(8,128)(2,1)S(1)}, u32[]{:S(2)}, u32[]{:S(2)}) %collective-permute-start.6) | collective-permute-done | bytes 1048608 | tf_op jit(solution)/shard_map/x/near_x/ppermute | solution.py:40
  110.9 18.4 %project.1 = (bf16[1024,2048]{1,0:T(8,128)(2,1)}, bf16[1024,2048]{1,0:T(8,128)(2,1)}, bf16[1024,768]{1,0:T(8,128)(2,1)}, bf16[2,1024,512]{2,1,0:T(8,128)(2,1)}, ...) custom-call(s32[2]{0:T(128)} %pad_add_fusion.where, ...), custom_call_target="tpu_custom_call" | custom-call | flops 7516192768 | bytes 31457280 | tf_op jit(solution)/shard_map/project/pallas_call | solution.py:225
  137.6 7.3 %attend.1 = (bf16[1024,1024]{1,0:T(8,128)(2,1)}, bf16[2,1024,128]{2,1,0:T(8,128)(2,1)}) custom-call(bf16[1024,768]{1,0:T(8,128)(2,1)} %get-tuple-element.40.q.kv, bf16[1024,768]{1,0:T(8,128)(2,1)} %get-tuple-element.40.q.kv, s32[1024,1]{1,0:T(8,128)} %copy.45.place_q, s32[1,1024]{1,0:T(1,128)} %bitcast.185, s32[1024,1]{1,0:T(8,128)} %copy.46.doc_q, ...), custom_call_target="tpu_custom_call" | custom-call | flops 1073741824 | bytes 5242880 | tf_op jit(solution)/shard_map/attend/pallas_call | solution.py:270
  144.9 11.0 %branches.1.rest_0_ = bf16[8,128,2048]{2,1,0:T(8,128)(2,1)} custom-call(s32[1]{0:T(128)} %bitcast.1.core, bf16[2,1024,512]{2,1,0:T(8,128)(2,1)} %get-tuple-element.39.act, bf16[2,1024,128]{2,1,0:T(8,128)(2,1)} %get-tuple-element.41.att, bf16[640,2048]{1,0:T(8,128)(2,1)} %constant_dynamic-update-slice_fusion.8.mine, bf16[640,2048]{1,0:T(8,128)(2,1)} %collective-permute-done.9.twin), custom_call_target="tpu_custom_call" | custom-call | flops 5368709120 | bytes 14680064 | tf_op jit(solution)/shard_map/branches/pallas_call | solution.py:392
  172.3 12.4 %branch_grad.1 = (bf16[2,1024,512]{2,1,0:T(8,128)(2,1)}, bf16[2,1024,128]{2,1,0:T(8,128)(2,1)}, f32[2,1,512]{2,1,0:T(1,128)}) custom-call(s32[1]{0:T(128)} %bitcast.1.core, bf16[1024,2048]{1,0:T(8,128)(2,1)} %add_dynamic-update-slice_fusion.g, bf16[640,2048]{1,0:T(8,128)(2,1)} %constant_dynamic-update-slice_fusion.8.mine, ...), custom_call_target="tpu_custom_call" | custom-call | flops 5368709120 | bytes 16777216 | tf_op jit(solution)/shard_map/branch_grad/pallas_call | solution.py:357
  188.6 11.3 %rows_grad.1 = (bf16[2,4,80,2048]{3,2,1,0:T(8,128)(2,1)}, bf16[2,4,80,2048]{3,2,1,0:T(8,128)(2,1)}) custom-call(s32[1]{0:T(128)} %bitcast.1.core, bf16[2,1024,512]{2,1,0:T(8,128)(2,1)} %get-tuple-element.39.act, bf16[2,1024,128]{2,1,0:T(8,128)(2,1)} %get-tuple-element.41.att, bf16[1024,2048]{1,0:T(8,128)(2,1)} %add_dynamic-update-slice_fusion.g, ...), custom_call_target="tpu_custom_call" | custom-call | flops 5368709120 | bytes 14680064 | tf_op jit(solution)/shard_map/rows_grad/pallas_call | solution.py:558
  214.3 9.2 %attend_back.1.g_mixed = bf16[1024,768]{1,0:T(8,128)(2,1)} custom-call(bf16[1024,768]{1,0:T(8,128)(2,1)} %get-tuple-element.40.q.kv, bf16[1024,768]{1,0:T(8,128)(2,1)} %get-tuple-element.40.q.kv, bf16[1024,1024]{1,0:T(8,128)(2,1)} %get-tuple-element.46.prob, bf16[2,1024,128]{2,1,0:T(8,128)(2,1)} %get-tuple-element.47.g, ...), custom_call_target="tpu_custom_call" | custom-call | flops 2147483648 | bytes 8388608 | tf_op jit(solution)/shard_map/attend_back/pallas_call | solution.py:319
  236.7 9.3 %half_grad.2 = (bf16[4,8,32,768]{3,2,1,0:T(8,128)(2,1)}, bf16[4,8,32,768]{3,2,1,0:T(8,128)(2,1)}) custom-call(s32[1]{0:T(128)} %bitcast.1.core, bf16[1024,2048]{1,0:T(8,128)(2,1)} %get-tuple-element.51.left, bf16[1,1024,768]{2,1,0:T(8,128)(2,1)} %bitcast.172, bf16[128,2048]{1,0:T(8,128)(2,1)} %get-tuple-element.104.rest_0_, bf16[2,4,80,2048]{3,2,1,0:T(8,128)(2,1)} %copy-done.3), custom_call_target="tpu_custom_call" | custom-call | flops 3221225472 | bytes 12582912 | tf_op jit(solution)/shard_map/half_grad/pallas_call | solution.py:524
  247.6 16.9 %collective-permute-start.25 = (bf16[128,2048]{1,0:T(8,128)(2,1)}, bf16[128,2048]{1,0:T(8,128)(2,1)}, u32[]{:S(2)}, u32[]{:S(2)}) collective-permute-start(bf16[128,2048]{1,0:T(8,128)(2,1)} %get-tuple-element.104.rest_0_), channel_id=1, source_target_pairs={{0,0},{16,1},{32,2},{48,3},{64,4},{80,5},{96,6},{112,7},{8,8},{24,... | collective-permute-start | bytes 1572872 | tf_op jit(solution)/shard_map/out/back/ppermute | solution.py:57
  264.5 10.5 %half_grad.3 = (bf16[4,8,32,1024]{3,2,1,0:T(8,128)(2,1)}, bf16[4,8,32,1024]{3,2,1,0:T(8,128)(2,1)}) custom-call(s32[1]{0:T(128)} %bitcast.1.core, bf16[1024,2048]{1,0:T(8,128)(2,1)} %get-tuple-element.50.left, bf16[2,1024,512]{2,1,0:T(8,128)(2,1)} %get-tuple-element.44.rest_0_.right.g_pre, bf16[4,8,32,768]{3,2,1,0:T(8,128)(2,1)} %get-tuple-element.53.rest_0_), custom_call_target="tpu_custom_call" | custom-call | flops 4294967296 | bytes 12582912 | tf_op jit(solution)/shard_map/half_grad/pallas_call | solution.py:524
  285.1 19.1 %partials.1 = bf16[8,144,2048]{2,1,0:T(8,128)(2,1)} custom-call(s32[10]{0:T(128)} %pad_add_fusion.1.where, bf16[1024,2048]{1,0:T(8,128)(2,1)} %constant_dynamic-update-slice_fusion.x, f32[4,2048]{1,0:T(4,128)} %get-tuple-element.49.norm, bf16[1024,768]{1,0:T(8,128)(2,1)} %attend_back.1.g_mixed, bf16[2,1024,512]{2,1,0:T(8,128)(2,1)} %get-tuple-element.44.rest_0_.right.g_pre, ...), custom_call_target="tpu_custom_call" | custom-call | flops 7516192768 | bytes 25165824 | tf_op jit(solution)/shard_map/partials/pallas_call | solution.py:480
  315.6 13.2 %collective-permute-done.44 = bf16[8,32,768]{2,1,0:T(8,128)(2,1)S(1)} collective-permute-done((bf16[8,32,768]{2,1,0:T(8,128)(2,1)S(1)}, bf16[8,32,768]{2,1,0:T(8,128)(2,1)S(1)}, u32[]{:S(2)}, u32[]{:S(2)}) %collective-permute-start.44) | collective-permute-done | bytes 393248 | tf_op jit(solution)/shard_map/qkv/z/ppermute | solution.py:40
  336.9 14.5 %collective-permute-done.31 = bf16[144,2048]{1,0:T(8,128)(2,1)S(1)} collective-permute-done((bf16[144,2048]{1,0:T(8,128)(2,1)S(1)}, bf16[144,2048]{1,0:T(8,128)(2,1)S(1)}, u32[]{:S(2)}, u32[]{:S(2)}) %collective-permute-start.31) | collective-permute-done | bytes 589856 | tf_op jit(solution)/shard_map/part/far_x/ppermute | solution.py:40
  357.9 6.3 %collective-permute-done.46 = bf16[8,32,1024]{2,1,0:T(8,128)(2,1)S(1)} collective-permute-done((bf16[8,32,1024]{2,1,0:T(8,128)(2,1)S(1)}, bf16[8,32,1024]{2,1,0:T(8,128)(2,1)S(1)}, u32[]{:S(2)}, u32[]{:S(2)}) %collective-permute-start.46) | collective-permute-done | bytes 524320 | tf_op jit(solution)/shard_map/up/z/ppermute | solution.py:40
  383.8 6.6 %all-to-all-start.1 = ((bf16[8,16,1792]{2,1,0:T(8,128)(2,1)}), bf16[8,16,1792]{2,1,0:T(8,128)(2,1)}, u32[]{:S(2)}, u32[]{:S(2)}) async-start(bf16[8,16,1792]{2,1,0:T(8,128)(2,1)} %fusion.25), calls=%async_computation.1 | async-start | bytes 917504 | tf_op jit(solution)/shard_map/columns/chips/all_to_all | solution.py:800
  407.9 7.7 %collective-permute-done.50 = bf16[8,16,1792]{2,1,0:T(8,128)(2,1)S(1)} collective-permute-done((bf16[8,16,1792]{2,1,0:T(8,128)(2,1)}, bf16[8,16,1792]{2,1,0:T(8,128)(2,1)S(1)}, u32[]{:S(2)}, u32[]{:S(2)}) %collective-permute-start.50) | collective-permute-done | bytes 458784 | tf_op jit(solution)/shard_map/columns/w_back/ppermute | solution.py:40
  425.2 16.2 %collective-permute-done.40 = f32[2,2048]{1,0:T(2,128)S(1)} collective-permute-done((f32[2,2048]{1,0:T(2,128)S(1)}, f32[2,2048]{1,0:T(2,128)S(1)}, u32[]{:S(2)}, u32[]{:S(2)}) %collective-permute-start.40) | collective-permute-done | bytes 16416 | tf_op jit(solution)/shard_map/small/w/ppermute | solution.py:40
  444.4 6.1 %rows_out.1 = (f32[512,2048]{1,0:T(8,128)}, f32[128,2048]{1,0:T(8,128)}) custom-call(s32[2]{0:T(128)} %pad_add_fusion.2.where, bf16[4,80,2048]{2,1,0:T(8,128)(2,1)} %copy-done.6, bf16[4,80,2048]{2,1,0:T(8,128)(2,1)} %copy-done.15), custom_call_target="tpu_custom_call" | custom-call | bytes 8388608 | tf_op jit(solution)/shard_map/rows_out/pallas_call | solution.py:625
  453.8 22.7 %collective-permute-done.36 = bf16[128,2048]{1,0:T(8,128)(2,1)S(1)} collective-permute-done((bf16[128,2048]{1,0:T(8,128)(2,1)}, bf16[128,2048]{1,0:T(8,128)(2,1)S(1)}, u32[]{:S(2)}, u32[]{:S(2)}) %collective-permute-start.36) | collective-permute-done | bytes 524320 | tf_op jit(solution)/shard_map/part/back/ppermute | solution.py:57
  476.6 7.1 %columns_out.1 = (f32[128,6144]{1,0:T(8,128)}, f32[128,8192]{1,0:T(8,128)}) custom-call(s32[2]{0:T(128)} %pad_add_fusion.2.where, bf16[2,8,16,1792]{3,2,1,0:T(8,128)(2,1)} %pad_maximum_fusion.5.refs_0_, bf16[2,8,16,1792]{3,2,1,0:T(8,128)(2,1)} %collective-permute-done.51.refs_1_, bf16[2,8,16,1792]{3,2,1,0:T(8,128)(2,1)} %collective-permute-done.52.refs_2_, ...), custom_call_target="tpu_custom_call" | custom-call | bytes 12582912 | tf_op jit(solution)/shard_map/columns_out/pallas_call | solution.py:595
  (307 shorter events, 198.6 us)
Async XLA Ops:
  13.2 30.9 %all-to-all-start = ((bf16[8,32,1920]{2,1,0:T(8,128)(2,1)}), bf16[8,32,1920]{2,1,0:T(8,128)(2,1)S(1)}, u32[]{:S(2)}, u32[]{:S(2)}) async-start(bf16[8,32,1920]{2,1,0:T(8,128)(2,1)} %copy.44), calls=%async_computation | async-start | bytes 1966080 | tf_op jit(solution)/shard_map/weights/all_to_all | solution.py:718
  19.2 91.7 %all-gather.3.cloned.1.call-start = ((), (), s32[]{:S(2)}) async-start(), calls=%async_computation.2 | async-start | bytes 8847360 | tf_op jit(solution)/shard_map/weights/all_gather | solution.py:719
  51.2 93.7 %collective-permute-start.9 = (bf16[640,2048]{1,0:T(8,128)(2,1)}, bf16[640,2048]{1,0:T(8,128)(2,1)}, u32[]{:S(2)}, u32[]{:S(2)}) collective-permute-start(bf16[640,2048]{1,0:T(8,128)(2,1)} %constant_dynamic-update-slice_fusion.8.mine), channel_id=1, source_target_pairs={{0,8},{8,0},{1,9},{9,1},{2,10},{10,2},{3,11},{11,3},{4,12},{12,4},... | collective-permute-start | bytes 7864328 | tf_op jit(solution)/shard_map/row_weights/ppermute | solution.py:40
  59.3 33.7 %collective-permute-start.11 = (bf16[128,2048]{1,0:T(8,128)(2,1)S(1)}, bf16[128,2048]{1,0:T(8,128)(2,1)S(1)}, u32[]{:S(2)}, u32[]{:S(2)}) collective-permute-start(bf16[128,2048]{1,0:T(8,128)(2,1)S(1)} %add_bitcast_fusion), channel_id=1, source_target_pairs={{0,0},{1,16},{2,32},{3,48},{4,64},{5,80},{6,96},{7,112},{8,8},{9,2... | collective-permute-start | bytes 1572872 | tf_op jit(solution)/shard_map/dy/ppermute | solution.py:53
  94.0 37.2 %collective-permute-start.13 = (bf16[128,2048]{1,0:T(8,128)(2,1)S(1)}, bf16[128,2048]{1,0:T(8,128)(2,1)}, u32[]{:S(2)}, u32[]{:S(2)}) collective-permute-start(bf16[128,2048]{1,0:T(8,128)(2,1)S(1)} %get-tuple-element.73), channel_id=1, source_target_pairs={{0,16},{16,32},{32,48},{48,0},{1,17},{17,33},{33,49},{49,1},{2,18}... | collective-permute-start | bytes 1572872 | tf_op jit(solution)/shard_map/dy/ring/ppermute | solution.py:40
  96.8 34.4 %collective-permute-start.12 = (bf16[128,2048]{1,0:T(8,128)(2,1)S(1)}, bf16[128,2048]{1,0:T(8,128)(2,1)}, u32[]{:S(2)}, u32[]{:S(2)}) collective-permute-start(bf16[128,2048]{1,0:T(8,128)(2,1)S(1)} %get-tuple-element.73), channel_id=1, source_target_pairs={{0,48},{16,0},{32,16},{48,32},{1,49},{17,1},{33,17},{49,33},{2,50}... | collective-permute-start | bytes 1572872 | tf_op jit(solution)/shard_map/dy/ring/ppermute | solution.py:40
  104.4 63.0 %collective-permute-start.16 = (bf16[128,2048]{1,0:T(8,128)(2,1)S(1)}, bf16[128,2048]{1,0:T(8,128)(2,1)}, u32[]{:S(2)}, u32[]{:S(2)}) collective-permute-start(bf16[128,2048]{1,0:T(8,128)(2,1)S(1)} %get-tuple-element.73), channel_id=1, source_target_pairs={{0,64},{4,68},{8,76},{12,72},{64,0},{68,4},{72,12},{76,8},{1,65},{... | collective-permute-start | bytes 1572872 | tf_op jit(solution)/shard_map/dy/own_x/ppermute | solution.py:40
  133.6 36.7 %collective-permute-start.17 = (bf16[256,2048]{1,0:T(8,128)(2,1)S(1)}, bf16[256,2048]{1,0:T(8,128)(2,1)S(1)}, u32[]{:S(2)}, u32[]{:S(2)}) collective-permute-start(bf16[256,2048]{1,0:T(8,128)(2,1)S(1)} %get-tuple-element.71), channel_id=1, source_target_pairs={{0,64},{4,68},{8,76},{12,72},{64,0},{68,4},{72,12},{76,8},{1,65},{... | collective-permute-start | bytes 3145736 | tf_op jit(solution)/shard_map/dy/near_x/ppermute | solution.py:40
  166.3 37.7 %collective-permute-start.19 = (bf16[2,128,2048]{2,1,0:T(8,128)(2,1)S(1)}, bf16[2,128,2048]{2,1,0:T(8,128)(2,1)}, u32[]{:S(2)}, u32[]{:S(2)}) collective-permute-start(bf16[2,128,2048]{2,1,0:T(8,128)(2,1)S(1)} %slice.202), channel_id=1, source_target_pairs={{0,64},{4,68},{8,76},{12,72},{64,0},{68,4},{72,12},{76,8},{1,65},{... | collective-permute-start | bytes 3145736 | tf_op jit(solution)/shard_map/out/near_x/ppermute | solution.py:40
  167.4 66.7 %collective-permute-start.10 = (bf16[128,2048]{1,0:T(8,128)(2,1)}, bf16[128,2048]{1,0:T(8,128)(2,1)}, u32[]{:S(2)}, u32[]{:S(2)}) collective-permute-start(bf16[128,2048]{1,0:T(8,128)(2,1)} %get-tuple-element.80), channel_id=1, source_target_pairs={{0,64},{4,68},{8,76},{12,72},{64,0},{68,4},{72,12},{76,8},{1,65},{... | collective-permute-start | bytes 1572872 | tf_op jit(solution)/shard_map/out/own_x/ppermute | solution.py:40
  230.3 46.8 %collective-permute-start.28 = (bf16[4,80,2048]{2,1,0:T(8,128)(2,1)}, bf16[4,80,2048]{2,1,0:T(8,128)(2,1)S(1)}, u32[]{:S(2)}, u32[]{:S(2)}) collective-permute-start(bf16[4,80,2048]{2,1,0:T(8,128)(2,1)} %dynamic-slice_bitcast_fusion), channel_id=1, source_target_pairs={{0,4},{4,0},{1,5},{5,1},{2,6},{6,2},{3,7},{7,3},{8,12},{12,8},{9,1... | collective-permute-start | bytes 3932168 | tf_op jit(solution)/shard_map/rows/w/ppermute | solution.py:40
  246.1 34.9 %collective-permute-start.27 = (bf16[4,8,32,768]{3,2,1,0:T(8,128)(2,1)}, bf16[4,8,32,768]{3,2,1,0:T(8,128)(2,1)}, u32[]{:S(2)}, u32[]{:S(2)}) collective-permute-start(bf16[4,8,32,768]{3,2,1,0:T(8,128)(2,1)} %get-tuple-element.53.rest_0_), channel_id=1, source_target_pairs={{0,8},{8,0},{1,9},{9,1},{2,10},{10,2},{3,11},{11,3},{4,12},{12,4},... | collective-permute-start | bytes 4718600 | tf_op jit(solution)/shard_map/qkv/core/ppermute | solution.py:40
  247.6 173.9 %collective-permute-start.25 = (bf16[128,2048]{1,0:T(8,128)(2,1)}, bf16[128,2048]{1,0:T(8,128)(2,1)}, u32[]{:S(2)}, u32[]{:S(2)}) collective-permute-start(bf16[128,2048]{1,0:T(8,128)(2,1)} %get-tuple-element.104.rest_0_), channel_id=1, source_target_pairs={{0,0},{16,1},{32,2},{48,3},{64,4},{80,5},{96,6},{112,7},{8,8},{24,... | collective-permute-start | bytes 1572872 | tf_op jit(solution)/shard_map/out/back/ppermute | solution.py:57
  276.2 56.5 %collective-permute-start.45 = (bf16[4,8,32,1024]{3,2,1,0:T(8,128)(2,1)}, bf16[4,8,32,1024]{3,2,1,0:T(8,128)(2,1)S(1)}, u32[]{:S(2)}, u32[]{:S(2)}) collective-permute-start(bf16[4,8,32,1024]{3,2,1,0:T(8,128)(2,1)} %get-tuple-element.54.rest_0_), channel_id=1, source_target_pairs={{0,8},{8,0},{1,9},{9,1},{2,10},{10,2},{3,11},{11,3},{4,12},{12,4},... | collective-permute-start | bytes 6291464 | tf_op jit(solution)/shard_map/up/core/ppermute | solution.py:40
  277.7 32.1 %collective-permute-start.56 = (bf16[80,2048]{1,0:T(8,128)(2,1)S(1)}, bf16[80,2048]{1,0:T(8,128)(2,1)S(1)}, u32[]{:S(2)}, u32[]{:S(2)}) collective-permute-start(bf16[80,2048]{1,0:T(8,128)(2,1)S(1)} %get-tuple-element.93), channel_id=1, source_target_pairs={{0,3},{1,0},{2,1},{3,2},{4,7},{5,4},{6,5},{7,6},{8,11},{9,8},{10,9... | collective-permute-start | bytes 983048 | tf_op jit(solution)/shard_map/rows/z/ppermute | solution.py:40
  281.0 31.1 %collective-permute-start.55 = (bf16[80,2048]{1,0:T(8,128)(2,1)S(1)}, bf16[80,2048]{1,0:T(8,128)(2,1)S(1)}, u32[]{:S(2)}, u32[]{:S(2)}) collective-permute-start(bf16[80,2048]{1,0:T(8,128)(2,1)S(1)} %get-tuple-element.94), channel_id=1, source_target_pairs={{0,2},{1,3},{2,0},{3,1},{4,6},{5,7},{6,4},{7,5},{8,10},{9,11},{10,... | collective-permute-start | bytes 983048 | tf_op jit(solution)/shard_map/rows/z/ppermute | solution.py:40
  281.0 33.4 %collective-permute-start.54 = (bf16[80,2048]{1,0:T(8,128)(2,1)S(1)}, bf16[80,2048]{1,0:T(8,128)(2,1)S(1)}, u32[]{:S(2)}, u32[]{:S(2)}) collective-permute-start(bf16[80,2048]{1,0:T(8,128)(2,1)S(1)} %get-tuple-element.92), channel_id=1, source_target_pairs={{0,1},{1,2},{2,3},{3,0},{4,5},{5,6},{6,7},{7,4},{8,9},{9,10},{10,1... | collective-permute-start | bytes 983048 | tf_op jit(solution)/shard_map/rows/z/ppermute | solution.py:40
  328.8 37.1 %collective-permute-start.30 = (bf16[2,144,2048]{2,1,0:T(8,128)(2,1)S(1)}, bf16[2,144,2048]{2,1,0:T(8,128)(2,1)S(1)}, u32[]{:S(2)}, u32[]{:S(2)}) collective-permute-start(bf16[2,144,2048]{2,1,0:T(8,128)(2,1)S(1)} %slice.215), channel_id=1, source_target_pairs={{0,64},{4,68},{8,76},{12,72},{64,0},{68,4},{72,12},{76,8},{1,65},{... | collective-permute-start | bytes 3538952 | tf_op jit(solution)/shard_map/part/near_x/ppermute | solution.py:40
  404.0 39.3 %collective-permute-start.60 = (bf16[4,80,2048]{2,1,0:T(8,128)(2,1)S(1)}, bf16[4,80,2048]{2,1,0:T(8,128)(2,1)S(1)}, u32[]{:S(2)}, u32[]{:S(2)}) collective-permute-start(bf16[4,80,2048]{2,1,0:T(8,128)(2,1)S(1)} %pad_maximum_fusion.1.mine), channel_id=1, source_target_pairs={{0,4},{4,0},{1,5},{5,1},{2,6},{6,2},{3,7},{7,3},{8,12},{12,8},{9,1... | collective-permute-start | bytes 3932168 | tf_op jit(solution)/shard_map/rows/w_back/ppermute | solution.py:40
  404.1 37.3 %collective-permute-start.40 = (f32[2,2048]{1,0:T(2,128)S(1)}, f32[2,2048]{1,0:T(2,128)S(1)}, u32[]{:S(2)}, u32[]{:S(2)}) collective-permute-start(f32[2,2048]{1,0:T(2,128)S(1)} %add_add_fusion.1), channel_id=1, source_target_pairs={{0,4},{4,0},{1,5},{5,1},{2,6},{6,2},{3,7},{7,3},{8,12},{12,8},{9,1... | collective-permute-start | bytes 49160 | tf_op jit(solution)/shard_map/small/w/ppermute | solution.py:40
  417.7 58.9 %collective-permute-start.51 = (bf16[2,8,16,1792]{3,2,1,0:T(8,128)(2,1)}, bf16[2,8,16,1792]{3,2,1,0:T(8,128)(2,1)}, u32[]{:S(2)}, u32[]{:S(2)}) collective-permute-start(bf16[2,8,16,1792]{3,2,1,0:T(8,128)(2,1)} %pad_maximum_fusion.5.refs_0_), channel_id=1, source_target_pairs={{0,1},{1,2},{2,3},{3,0},{4,5},{5,6},{6,7},{7,4},{8,9},{9,10},{10,1... | collective-permute-start | bytes 2752520 | tf_op jit(solution)/shard_map/columns/z_back/ppermute | solution.py:40
  420.2 56.3 %collective-permute-start.52 = (bf16[2,8,16,1792]{3,2,1,0:T(8,128)(2,1)}, bf16[2,8,16,1792]{3,2,1,0:T(8,128)(2,1)}, u32[]{:S(2)}, u32[]{:S(2)}) collective-permute-start(bf16[2,8,16,1792]{3,2,1,0:T(8,128)(2,1)} %pad_maximum_fusion.5.refs_0_), channel_id=1, source_target_pairs={{0,2},{1,3},{2,0},{3,1},{4,6},{5,7},{6,4},{7,5},{8,10},{9,11},{10,... | collective-permute-start | bytes 2752520 | tf_op jit(solution)/shard_map/columns/z_back/ppermute | solution.py:40
  421.4 55.1 %collective-permute-start.53 = (bf16[2,8,16,1792]{3,2,1,0:T(8,128)(2,1)}, bf16[2,8,16,1792]{3,2,1,0:T(8,128)(2,1)}, u32[]{:S(2)}, u32[]{:S(2)}) collective-permute-start(bf16[2,8,16,1792]{3,2,1,0:T(8,128)(2,1)} %pad_maximum_fusion.5.refs_0_), channel_id=1, source_target_pairs={{0,3},{1,0},{2,1},{3,2},{4,7},{5,4},{6,5},{7,6},{8,11},{9,8},{10,9... | collective-permute-start | bytes 2752520 | tf_op jit(solution)/shard_map/columns/z_back/ppermute | solution.py:40
  441.4 35.2 %collective-permute-start.36 = (bf16[128,2048]{1,0:T(8,128)(2,1)}, bf16[128,2048]{1,0:T(8,128)(2,1)S(1)}, u32[]{:S(2)}, u32[]{:S(2)}) collective-permute-start(bf16[128,2048]{1,0:T(8,128)(2,1)} %fusion.13), channel_id=1, source_target_pairs={{0,0},{16,1},{32,2},{48,3},{64,4},{80,5},{96,6},{112,7},{8,8},{24,... | collective-permute-start | bytes 1572872 | tf_op jit(solution)/shard_map/part/back/ppermute | solution.py:57
  (73 other events, 1032.5 us)
Sparse Core Ops, SparseCore 0:
  45.3 59.4 all-gather.2
